TPU v7x, 512 devices: a whole 4x4x16 slice. The times are simulated.
512 devices in a mesh: sec: 128 (over z, y, core), tile: 4 (over x).
Axes of the slice: x: 4, y: 4, z: 16, core: 2. Of those that a mesh axis runs over, the one named last changes fastest.
Arguments:
- pixels: bfloat16 [128, 128, 4096], P('sec', 'tile'), may hold values from -6 to 6
- offsets: int32 [2, 2, 128, 128], P(None, None, 'sec', 'tile'), may hold values from -8 to 8
- connections: int32 [4, 128, 128], P(None, 'sec', 'tile'), may hold values from 0 to 127
- confidence: float32 [128, 128], P('sec', 'tile'), may hold values from 0.3 to 3
Outputs:
- measured: float32 [2, 2, 128, 128], P(None, None, 'sec', 'tile')
- displacement: float32 [2, 128, 128], P(None, 'sec', 'tile')
All inputs are finite; a program needn't handle non-finite values.
Results may differ from a plain program's by a relative error of at most 0.00065.
Values may be sent and summed in bfloat16 or wider, within the bound.
No kernel may reach another device: no remote copies, remote signals or barrier semaphores. Data moves between devices by JAX's collectives and lax.ppermute only.
A program may use at most 64 MiB of HBM per device.

v0:
```python
import math

import jax
import jax.numpy as jnp
from jax import lax
from jax.sharding import PartitionSpec as P

PIX = 64
ITERS = 3


stiff_plane = 1.0
anchor = 0.05
springs = ((1, 1.0), (2, 0.5))


def passed_along(array, axis, by):
    count = lax.axis_size(axis)
    pairs = [(i, i + by) for i in range(count) if 0 <= i + by < count]
    return lax.ppermute(array, axis, pairs)


def tables():
    positions = jnp.arange(PIX, dtype=jnp.int32)
    angles = jnp.mod(positions[:, None] * positions[None, :], PIX).astype(jnp.float32) * (
        2.0 * math.pi / PIX
    )
    cosine = jnp.cos(angles)
    sine = jnp.sin(angles)
    row_table = jnp.concatenate([cosine, sine], 1).astype(jnp.bfloat16)
    col_table = jnp.concatenate([cosine, sine], 0).astype(jnp.bfloat16)
    return (row_table, col_table)


def spectrum(patches, row_table, col_table):
    patch_count = patches.shape[0]
    rows = patches.reshape(patch_count * PIX, PIX)
    half_done = jnp.dot(rows, row_table, preferred_element_type=jnp.float32).astype(jnp.bfloat16)
    half_done = half_done.reshape(patch_count, PIX, 2 * PIX)
    full = jnp.einsum("km,bmc->bkc", col_table, half_done, preferred_element_type=jnp.float32)
    real_part = full[:, :PIX, :PIX] - full[:, PIX:, PIX:]
    imag_part = -(full[:, :PIX, PIX:] + full[:, PIX:, :PIX])
    return jnp.concatenate([real_part, imag_part], -1).astype(jnp.bfloat16)


def phases(shift_by):
    positions = jnp.arange(PIX, dtype=jnp.int32)
    nudges = jnp.array([-1, 0, 1], dtype=jnp.int32)
    target = shift_by[:, None] + nudges[None, :]
    angles = jnp.mod(target[:, :, None] * positions[None, None, :], PIX).astype(jnp.float32) * (
        2.0 * math.pi / PIX
    )
    return (jnp.cos(angles), jnp.sin(angles))


def patch_scores(spec_a, spec_b, offset_pair):
    full_a = spec_a.astype(jnp.float32)
    full_b = spec_b.astype(jnp.float32)
    energy_a = jnp.sum(full_a * full_a, axis=(1, 2)) / PIX**4 + 1e-05
    energy_b = jnp.sum(full_b * full_b, axis=(1, 2)) / PIX**4 + 1e-05
    real_a, imag_a = (full_a[..., :PIX], full_a[..., PIX:])
    real_b, imag_b = (full_b[..., :PIX], full_b[..., PIX:])
    cross = jnp.concatenate(
        [real_a * real_b + imag_a * imag_b, imag_a * real_b - real_a * imag_b], -1
    )
    cos_col, sin_col = phases(offset_pair[1])
    upper = jnp.concatenate([cos_col, sin_col], 1)
    lower = jnp.concatenate([-sin_col, cos_col], 1)
    phase_table = jnp.concatenate([upper, lower], 2)
    partial_sum = jnp.einsum("bkc,bgc->bkg", cross, phase_table, precision=lax.Precision.HIGHEST)
    cos_row, sin_row = phases(offset_pair[0])
    corr = jnp.einsum(
        "bfk,bke->bfe", cos_row, partial_sum[..., :3], precision=lax.Precision.HIGHEST
    )
    corr = corr - jnp.einsum(
        "bfk,bke->bfe", sin_row, partial_sum[..., 3:], precision=lax.Precision.HIGHEST
    )
    corr = corr / PIX**2
    score = corr / (PIX * jnp.sqrt(energy_a * energy_b))[:, None, None]
    weights = score * score
    summed = 1.0 + jnp.sum(weights, axis=(1, 2))
    nudges = jnp.array([-1.0, 0.0, 1.0], dtype=jnp.float32)
    along_rows = jnp.sum(weights * nudges[None, :, None], axis=(1, 2)) / summed
    along_cols = jnp.sum(weights * nudges[None, None, :], axis=(1, 2)) / summed
    return jnp.stack(
        [
            offset_pair[0].astype(jnp.float32) + along_rows,
            offset_pair[1].astype(jnp.float32) + along_cols,
        ]
    )


def on_device(pixels, offsets, connections, confidence):
    patch_count = pixels.shape[1]
    block_size = math.gcd(patch_count, 32)
    groups = patch_count // block_size
    row_table, col_table = tables()

    def spectra_of(local):
        grouped = local.reshape(groups, block_size, PIX * PIX)
        done = lax.map(lambda piece: spectrum(piece, row_table, col_table), grouped)
        return done.reshape(patch_count, PIX, 2 * PIX)

    own_spec = spectra_of(pixels[0])
    earlier = []
    for distance in (1, 2):
        shifted = passed_along(pixels, "sec", distance)
        earlier.append(spectra_of(shifted[0]))

    def scored(spec_b, offset_pair):
        grouped_a = own_spec.reshape(groups, block_size, PIX, 2 * PIX)
        grouped_b = spec_b.reshape(groups, block_size, PIX, 2 * PIX)
        grouped_off = jnp.transpose(offset_pair.reshape(2, groups, block_size), (1, 0, 2))
        done = lax.map(
            lambda parts: patch_scores(parts[0], parts[1], parts[2]),
            (grouped_a, grouped_b, grouped_off),
        )
        return jnp.transpose(done, (1, 0, 2)).reshape(2, patch_count)

    measured = jnp.stack(
        [scored(earlier[0], offsets[0, :, 0]), scored(earlier[1], offsets[1, :, 0])]
    )[:, :, None, :]
    section = lax.axis_index("sec")
    packed = jnp.concatenate([confidence[None], measured.reshape(4, 1, patch_count)], 0)
    ahead_of = {}
    for distance in (1, 2):
        ahead_of[distance] = passed_along(packed, "sec", -distance)
    rest = jnp.zeros((2, 1, patch_count), jnp.float32)
    for distance, spring in springs:
        in_chain = (section >= distance).astype(jnp.float32)
        ahead_rest = ahead_of[distance][1 + 2 * (distance - 1) : 3 + 2 * (distance - 1)]
        rest = rest + spring * (
            in_chain * confidence * measured[distance - 1] - ahead_of[distance][0] * ahead_rest
        )
    node_links = connections[:, 0]
    displacement = jnp.zeros((2, 1, patch_count), jnp.float32)
    gradient = -rest
    for step_index in range(ITERS):
        grad_sq = lax.psum(jnp.sum(gradient * gradient), ("sec", "tile"))
        gathered = lax.all_gather(gradient, "tile", axis=2, tiled=True)
        every_value = gathered[:, 0]
        neighbours = every_value[:, node_links]
        differ = gradient[:, 0][:, None] - neighbours
        pulled = (
            jnp.zeros((2, gathered.shape[2]), jnp.float32)
            .at[:, node_links.reshape(-1)]
            .add(-differ.reshape(2, -1))
        )
        pulled_own = lax.psum_scatter(pulled[:, None], "tile", scatter_dimension=2, tiled=True)
        result = stiff_plane * (differ.sum(1)[:, None] + pulled_own) + anchor * gradient
        nearby = {}
        for hop_count in (1, 2, -1, -2):
            nearby[hop_count] = passed_along(gradient, "sec", hop_count)
        for hessian_distance, hessian_spring in springs:
            hessian_in_chain = (section >= hessian_distance).astype(jnp.float32)
            own_term = hessian_in_chain * confidence * (gradient - nearby[hessian_distance])
            next_term = ahead_of[hessian_distance][0] * (nearby[-hessian_distance] - gradient)
            result = result + hessian_spring * (own_term - next_term)
        grad_curve = lax.psum(jnp.sum(gradient * result), ("sec", "tile"))
        alpha = grad_sq / grad_curve
        displacement = displacement - alpha * gradient
        gradient = gradient - alpha * result
    return (measured, displacement)


def solution(mesh):
    return jax.shard_map(
        on_device,
        mesh=mesh,
        in_specs=(
            P("sec", "tile", None),
            P(None, None, "sec", "tile"),
            P(None, "sec", "tile"),
            P("sec", "tile"),
        ),
        out_specs=(P(None, None, "sec", "tile"), P(None, "sec", "tile")),
        check_vma=False,
    )
```

profile of v0, /device:TPU:1, one launch (start us, length us, event | category | flops | bytes accessed | tf_op | source)
XLA Modules:
  0.0 498.1 jit_solution(12897143819472126058)
XLA Ops:
  7.2 4.0 collective-permute-start.1
  11.3 4.0 collective-permute-start
  15.5 1.5 reshape.524
  17.5 1.3 reduce.3
  18.9 0.5 fusion.99
  19.4 0.7 compare_select_fusion
  20.1 0.6 reshape.532
  20.7 0.7 slice_bitcast_fusion.3
  22.0 0.6 convolution_bitcast_fusion.2
  22.6 0.6 fusion.17
  23.9 0.6 multiply_reduce_fusion.2
  24.5 1.8 fusion.73
  26.4 0.5 reshape.526
  27.5 0.6 convolution_bitcast_fusion.1
  28.1 0.6 fusion.14
  28.7 0.6 multiply_reduce_fusion.1
  29.6 0.5 reshape.528
  30.7 0.6 convolution_bitcast_fusion
  31.3 0.6 fusion.11
  31.9 0.6 multiply_reduce_fusion
  32.8 1.0 multiply_add_fusion
  33.8 1.9 fusion.22
  35.7 0.9 fusion.53
  36.7 0.9 fusion.5
  37.6 1.9 fusion.18
  39.5 0.9 fusion.56
  40.5 1.5 multiply_reduce_fusion.6
  42.1 1.3 collective-permute-start.3
  43.4 3.3 collective-permute-start.2
  46.8 3.5 collective-permute-done.2
  50.5 9.3 %all_gather.9 = f32[2,1,128]{0,1,2:T(1,128)S(1)} all-gather(f32[2,1,32]{0,1,2:T(1,128)S(1)} %copy.132), channel_id=1, replica_groups=mesh['sec'=128,'tile'=4] {'tile'}, dimensions={2}, use_global_device_ids=true | all-gather | bytes 1280 | tf_op jit(solution)/shard_map/all_gather | solution.py:140
  59.8 0.6 gather_fusion
  60.4 1.7 scatter_custom_fusion
  62.2 2.1 collective-permute-start.6
  64.3 5.1 %collective-permute-start.4 = (f32[2,1,32]{2,0,1:T(2,128)S(1)}, f32[2,1,32]{2,0,1:T(2,128)S(1)}, u32[]{:S(2)}, u32[]{:S(2)}) collective-permute-start(f32[2,1,32]{2,0,1:T(2,128)S(1)} %get-tuple-element.130), channel_id=1, source_target_pairs={{0,4},{4,8},{8,12},{12,16},{16,20},{20,24},{24,28},{28,32},{32,36}... | collective-permute-start | bytes 776 | tf_op jit(solution)/shard_map/ppermute | solution.py:20
  69.4 1.3 collective-permute-start.7
  70.7 1.9 collective-permute-start.5
  72.8 20.8 %reduce-scatter.10.cloned.1.call-done = f32[32,2]{1,0:T(8,128)} async-done(((f32[128,2]{1,0:T(8,128)}), f32[32,2]{1,0:T(8,128)}) %reduce-scatter.10.cloned.1.call-update) | async-done | bytes 272
  93.6 0.8 copy.146
  94.4 0.7 multiply_reduce_fusion.10
  95.1 106.3 %all-reduce.2 = (f32[]{:T(128)}, f32[]{:T(128)}) all-reduce(f32[]{:T(128)} %get-tuple-element.110, f32[]{:T(128)} %get-tuple-element.109), channel_id=1, replica_groups=mesh['sec'=128,'tile'=4] {'sec','tile'}, use_global_device_ids=true, to_apply=%region_10.11 | all-reduce | flops 2 | bytes 16 | tf_op jit(solution)/shard_map/psum | solution.py:139
  202.9 9.0 %all_gather.10 = f32[2,1,128]{0,1,2:T(1,128)S(1)} all-gather(f32[2,1,32]{0,1,2:T(1,128)S(1)} %copy.136), channel_id=1, replica_groups=mesh['sec'=128,'tile'=4] {'tile'}, dimensions={2}, use_global_device_ids=true | all-gather | bytes 1280 | tf_op jit(solution)/shard_map/all_gather | solution.py:140
  211.9 0.6 gather_fusion.1
  212.6 1.7 scatter_custom_fusion.1
  214.3 1.3 collective-permute-start.10
  215.6 5.9 %collective-permute-start.9 = (f32[2,1,32]{2,0,1:T(2,128)S(1)}, f32[2,1,32]{2,0,1:T(2,128)S(1)}, u32[]{:S(2)}, u32[]{:S(2)}) collective-permute-start(f32[2,1,32]{2,0,1:T(2,128)S(1)} %multiply_subtract_fusion.4), channel_id=1, source_target_pairs={{4,0},{8,4},{12,8},{16,12},{20,16},{24,20},{28,24},{32,28},{36,32}... | collective-permute-start | bytes 776 | tf_op jit(solution)/shard_map/ppermute | solution.py:20
  221.5 3.2 collective-permute-start.8
  224.7 1.3 collective-permute-start.11
  226.1 11.6 %reduce-scatter.12.cloned.1.call-done = f32[32,2]{1,0:T(8,128)} async-done(((f32[128,2]{1,0:T(8,128)}), f32[32,2]{1,0:T(8,128)}) %reduce-scatter.12.cloned.1.call-update) | async-done | bytes 272
  237.8 0.8 copy.148
  238.6 0.7 multiply_reduce_fusion.8
  239.3 106.3 %all-reduce.1 = (f32[]{:T(128)}, f32[]{:T(128)}) all-reduce(f32[]{:T(128)} %get-tuple-element.108, f32[]{:T(128)} %get-tuple-element.99), channel_id=1, replica_groups=mesh['sec'=128,'tile'=4] {'sec','tile'}, use_global_device_ids=true, to_apply=%region_17.18 | all-reduce | flops 2 | bytes 16 | tf_op jit(solution)/shard_map/psum | solution.py:139
  347.1 9.0 %all_gather.11 = f32[2,1,128]{0,1,2:T(1,128)S(1)} all-gather(f32[2,1,32]{0,1,2:T(1,128)S(1)} %copy.140), channel_id=1, replica_groups=mesh['sec'=128,'tile'=4] {'tile'}, dimensions={2}, use_global_device_ids=true | all-gather | bytes 1280 | tf_op jit(solution)/shard_map/all_gather | solution.py:140
  356.0 0.6 gather_fusion.2
  356.7 1.7 scatter_custom_fusion.2
  358.4 5.9 %collective-permute-start.13 = (f32[2,1,32]{2,0,1:T(2,128)S(1)}, f32[2,1,32]{2,0,1:T(2,128)S(1)}, u32[]{:S(2)}, u32[]{:S(2)}) collective-permute-start(f32[2,1,32]{2,0,1:T(2,128)S(1)} %multiply_subtract_fusion.3), channel_id=1, source_target_pairs={{4,0},{8,4},{12,8},{16,12},{20,16},{24,20},{28,24},{32,28},{36,32}... | collective-permute-start | bytes 776 | tf_op jit(solution)/shard_map/ppermute | solution.py:20
  364.4 1.3 collective-permute-start.15
  365.7 3.5 collective-permute-start.12
  369.2 2.4 collective-permute-start.14
  371.7 10.2 %reduce-scatter.14.cloned.1.call-done = f32[32,2]{1,0:T(8,128)} async-done(((f32[128,2]{1,0:T(8,128)}), f32[32,2]{1,0:T(8,128)}) %reduce-scatter.14.cloned.1.call-update) | async-done | bytes 272
  381.9 0.8 copy.150
  382.7 0.7 fusion.98
  383.4 106.3 %all-reduce = (f32[]{:T(128)}, f32[]{:T(128)}) all-reduce(f32[]{:T(128)} %get-tuple-element.98, f32[]{:T(128)} %get-tuple-element.97), channel_id=1, replica_groups=mesh['sec'=128,'tile'=4] {'sec','tile'}, use_global_device_ids=true, to_apply=%region_24.25 | all-reduce | flops 2 | bytes 16 | tf_op jit(solution)/shard_map/psum | solution.py:139
  491.0 0.6 multiply_subtract_fusion.2
  (76 shorter events, 4.9 us)
Async XLA Ops:
  7.2 86.4 %reduce-scatter.10.cloned.1.call-start = ((), (), s32[]{:S(2)}) async-start(), calls=%async_computation.3 | async-start | bytes 81920
  7.2 22.3 %collective-permute-start.1 = (bf16[1,32,4096]{2,1,0:T(8,128)(2,1)}, bf16[1,32,4096]{2,1,0:T(8,128)(2,1)S(1)}, u32[]{:S(2)}, u32[]{:S(2)}) collective-permute-start(bf16[1,32,4096]{2,1,0:T(8,128)(2,1)} %param.10), channel_id=1, source_target_pairs={{0,8},{4,12},{8,16},{12,20},{16,24},{20,28},{24,32},{28,36},{32,40... | collective-permute-start | bytes 786440 | tf_op jit(solution)/shard_map/ppermute | solution.py:20
  11.3 15.1 %collective-permute-start = (bf16[1,32,4096]{2,1,0:T(8,128)(2,1)}, bf16[1,32,4096]{2,1,0:T(8,128)(2,1)S(1)}, u32[]{:S(2)}, u32[]{:S(2)}) collective-permute-start(bf16[1,32,4096]{2,1,0:T(8,128)(2,1)} %param.10), channel_id=1, source_target_pairs={{0,4},{4,8},{8,12},{12,16},{16,20},{20,24},{24,28},{28,32},{32,36}... | collective-permute-start | bytes 786440 | tf_op jit(solution)/shard_map/ppermute | solution.py:20
  23.2 0.7 copy-start.4
  23.2 0.7 copy-start.6
  32.7 1.0 copy-start
  36.6 3.8 copy-start.7
  37.6 4.4 copy-start.1
  37.6 4.5 copy-start.5
  37.6 5.8 %copy-start.3 = (s32[128]{0:T(128)S(1)}, s32[128]{0:T(128)}, u32[]{:S(2)}) copy-start(s32[128]{0:T(128)} %reshape.532) | copy-start | bytes 1540
  42.1 449.5 %copy-start.2 = (f32[2,2,32]{2,1,0:T(2,128)}, f32[2,2,32]{2,1,0:T(2,128)S(1)}, u32[]{:S(2)}) copy-start(f32[2,2,32]{2,1,0:T(2,128)S(1)} %pad_maximum_fusion.5) | copy-start | bytes 1540
  42.1 4.7 collective-permute-start.3
  43.4 6.9 %collective-permute-start.2 = (f32[5,1,32]{2,0,1:T(8,128)S(1)}, f32[5,1,32]{2,0,1:T(8,128)S(1)}, u32[]{:S(2)}, u32[]{:S(2)}) collective-permute-start(f32[5,1,32]{2,0,1:T(8,128)S(1)} %pad_maximum_fusion.4), channel_id=1, source_target_pairs={{4,0},{8,4},{12,8},{16,12},{20,16},{24,20},{28,24},{32,28},{36,32}... | collective-permute-start | bytes 1928 | tf_op jit(solution)/shard_map/ppermute | solution.py:20
  62.2 175.6 %reduce-scatter.12.cloned.1.call-start = ((), (), s32[]{:S(2)}) async-start(), calls=%async_computation.4 | async-start | bytes 81920
  62.2 32.2 %collective-permute-start.6 = (f32[2,1,32]{2,0,1:T(2,128)S(1)}, f32[2,1,32]{2,0,1:T(2,128)S(1)}, u32[]{:S(2)}, u32[]{:S(2)}) collective-permute-start(f32[2,1,32]{2,0,1:T(2,128)S(1)} %get-tuple-element.130), channel_id=1, source_target_pairs={{0,8},{4,12},{8,16},{12,20},{16,24},{20,28},{24,32},{28,36},{32,40... | collective-permute-start | bytes 776 | tf_op jit(solution)/shard_map/ppermute | solution.py:20
  64.3 30.1 %collective-permute-start.4 = (f32[2,1,32]{2,0,1:T(2,128)S(1)}, f32[2,1,32]{2,0,1:T(2,128)S(1)}, u32[]{:S(2)}, u32[]{:S(2)}) collective-permute-start(f32[2,1,32]{2,0,1:T(2,128)S(1)} %get-tuple-element.130), channel_id=1, source_target_pairs={{0,4},{4,8},{8,12},{12,16},{16,20},{20,24},{24,28},{28,32},{32,36}... | collective-permute-start | bytes 776 | tf_op jit(solution)/shard_map/ppermute | solution.py:20
  69.4 24.9 %collective-permute-start.7 = (f32[2,1,32]{2,0,1:T(2,128)S(1)}, f32[2,1,32]{2,0,1:T(2,128)S(1)}, u32[]{:S(2)}, u32[]{:S(2)}) collective-permute-start(f32[2,1,32]{2,0,1:T(2,128)S(1)} %get-tuple-element.130), channel_id=1, source_target_pairs={{8,0},{12,4},{16,8},{20,12},{24,16},{28,20},{32,24},{36,28},{40,32... | collective-permute-start | bytes 776 | tf_op jit(solution)/shard_map/ppermute | solution.py:20
  70.7 23.7 %collective-permute-start.5 = (f32[2,1,32]{2,0,1:T(2,128)S(1)}, f32[2,1,32]{2,0,1:T(2,128)S(1)}, u32[]{:S(2)}, u32[]{:S(2)}) collective-permute-start(f32[2,1,32]{2,0,1:T(2,128)S(1)} %get-tuple-element.130), channel_id=1, source_target_pairs={{4,0},{8,4},{12,8},{16,12},{20,16},{24,20},{28,24},{32,28},{36,32}... | collective-permute-start | bytes 776 | tf_op jit(solution)/shard_map/ppermute | solution.py:20
  214.3 167.6 %reduce-scatter.14.cloned.1.call-start = ((), (), s32[]{:S(2)}) async-start(), calls=%async_computation.5 | async-start | bytes 81920
  214.3 24.2 %collective-permute-start.10 = (f32[2,1,32]{2,0,1:T(2,128)S(1)}, f32[2,1,32]{2,0,1:T(2,128)S(1)}, u32[]{:S(2)}, u32[]{:S(2)}) collective-permute-start(f32[2,1,32]{2,0,1:T(2,128)S(1)} %multiply_subtract_fusion.4), channel_id=1, source_target_pairs={{0,8},{4,12},{8,16},{12,20},{16,24},{20,28},{24,32},{28,36},{32,40... | collective-permute-start | bytes 776 | tf_op jit(solution)/shard_map/ppermute | solution.py:20
  215.6 22.9 %collective-permute-start.9 = (f32[2,1,32]{2,0,1:T(2,128)S(1)}, f32[2,1,32]{2,0,1:T(2,128)S(1)}, u32[]{:S(2)}, u32[]{:S(2)}) collective-permute-start(f32[2,1,32]{2,0,1:T(2,128)S(1)} %multiply_subtract_fusion.4), channel_id=1, source_target_pairs={{4,0},{8,4},{12,8},{16,12},{20,16},{24,20},{28,24},{32,28},{36,32}... | collective-permute-start | bytes 776 | tf_op jit(solution)/shard_map/ppermute | solution.py:20
  221.5 17.0 %collective-permute-start.8 = (f32[2,1,32]{2,0,1:T(2,128)S(1)}, f32[2,1,32]{2,0,1:T(2,128)S(1)}, u32[]{:S(2)}, u32[]{:S(2)}) collective-permute-start(f32[2,1,32]{2,0,1:T(2,128)S(1)} %multiply_subtract_fusion.4), channel_id=1, source_target_pairs={{0,4},{4,8},{8,12},{12,16},{16,20},{20,24},{24,28},{28,32},{32,36}... | collective-permute-start | bytes 776 | tf_op jit(solution)/shard_map/ppermute | solution.py:20
  224.7 13.8 %collective-permute-start.11 = (f32[2,1,32]{2,0,1:T(2,128)S(1)}, f32[2,1,32]{2,0,1:T(2,128)S(1)}, u32[]{:S(2)}, u32[]{:S(2)}) collective-permute-start(f32[2,1,32]{2,0,1:T(2,128)S(1)} %multiply_subtract_fusion.4), channel_id=1, source_target_pairs={{8,0},{12,4},{16,8},{20,12},{24,16},{28,20},{32,24},{36,28},{40,32... | collective-permute-start | bytes 776 | tf_op jit(solution)/shard_map/ppermute | solution.py:20
  358.4 24.3 %collective-permute-start.13 = (f32[2,1,32]{2,0,1:T(2,128)S(1)}, f32[2,1,32]{2,0,1:T(2,128)S(1)}, u32[]{:S(2)}, u32[]{:S(2)}) collective-permute-start(f32[2,1,32]{2,0,1:T(2,128)S(1)} %multiply_subtract_fusion.3), channel_id=1, source_target_pairs={{4,0},{8,4},{12,8},{16,12},{20,16},{24,20},{28,24},{32,28},{36,32}... | collective-permute-start | bytes 776 | tf_op jit(solution)/shard_map/ppermute | solution.py:20
  364.4 18.3 %collective-permute-start.15 = (f32[2,1,32]{2,0,1:T(2,128)S(1)}, f32[2,1,32]{2,0,1:T(2,128)S(1)}, u32[]{:S(2)}, u32[]{:S(2)}) collective-permute-start(f32[2,1,32]{2,0,1:T(2,128)S(1)} %multiply_subtract_fusion.3), channel_id=1, source_target_pairs={{8,0},{12,4},{16,8},{20,12},{24,16},{28,20},{32,24},{36,28},{40,32... | collective-permute-start | bytes 776 | tf_op jit(solution)/shard_map/ppermute | solution.py:20
  365.7 17.0 %collective-permute-start.12 = (f32[2,1,32]{2,0,1:T(2,128)S(1)}, f32[2,1,32]{2,0,1:T(2,128)S(1)}, u32[]{:S(2)}, u32[]{:S(2)}) collective-permute-start(f32[2,1,32]{2,0,1:T(2,128)S(1)} %multiply_subtract_fusion.3), channel_id=1, source_target_pairs={{0,4},{4,8},{8,12},{12,16},{16,20},{20,24},{24,28},{28,32},{32,36}... | collective-permute-start | bytes 776 | tf_op jit(solution)/shard_map/ppermute | solution.py:20
  369.2 13.5 %collective-permute-start.14 = (f32[2,1,32]{2,0,1:T(2,128)S(1)}, f32[2,1,32]{2,0,1:T(2,128)S(1)}, u32[]{:S(2)}, u32[]{:S(2)}) collective-permute-start(f32[2,1,32]{2,0,1:T(2,128)S(1)} %multiply_subtract_fusion.3), channel_id=1, source_target_pairs={{0,8},{4,12},{8,16},{12,20},{16,24},{20,28},{24,32},{28,36},{32,40... | collective-permute-start | bytes 776 | tf_op jit(solution)/shard_map/ppermute | solution.py:20
Sparse Core Ops, SparseCore 0:
  62.3 31.2 reduce-scatter.9
  214.4 23.2 reduce-scatter.11
  358.5 23.2 reduce-scatter.13
where the time goes:
time: 500 us; the launch traced here: 498 us
  blocking collectives  346 us (69%)
  starting transfers between devices  48 us (10%)
  waiting for transfers between devices  46.3 us (9%)
  between operations  18.2 us (4%)
  other arithmetic  18 us (4%)
  local copies, waits for them, and re-layouts  10.8 us (2%)
  matrix products  10.7 us (2%)
    psum x3, blocking collectives, on_device(): grad_sq = lax.psum(jnp.sum(gradient * gradient), ('sec', 'tile'))  319 us
    ppermute x16, starting transfers between devices, passed_along(): return lax.ppermute(array, axis, pairs)  47.9 us
    unnamed x6, waiting for transfers between devices  42.8 us
    all_gather x3, blocking collectives, on_device(): gathered = lax.all_gather(gradient, 'tile', axis=2, tiled=True)  27.2 us
  transfers between devices with their start and end apart: 19, of which 4 were waited for; matrix products, arithmetic and copies ran while one was open for 3% of the time, Pallas kernels for 0%

commit v1 on v0

v1 whole, which is shorter than its diff:
```python
import jax
import jax.numpy as jnp
from jax import lax
from jax.experimental import pallas as pl
from jax.experimental.pallas import tpu as pltpu
from jax.sharding import Mesh
from jax.sharding import PartitionSpec as P

PIX = 64
LANES = 128
TILES = PIX * PIX // LANES
REACH = 4
ROWS = 16
PLANE = 8
WINDOW = 3 * PLANE
ANCHOR = 0.05
SPRINGS = ((1, 1.0), (2, 0.5))
SEC = ("z", "y", "core")
VMEM = pl.BlockSpec(memory_space=pltpu.VMEM)
SMEM = pl.BlockSpec(memory_space=pltpu.SMEM)


def lanes_of(rows):
    return lax.broadcasted_iota(jnp.int32, (rows, LANES), 1)


def sublanes_of(rows):
    return lax.broadcasted_iota(jnp.int32, (rows, LANES), 0)


def pick(values, index):
    return jnp.take_along_axis(values, index, axis=1, mode="promise_in_bounds")


def pick_rows(values, index):
    parts = [pick(values[8 * i : 8 * i + 8], index[8 * i : 8 * i + 8]) for i in range(values.shape[0] // 8)]
    return jnp.concatenate(parts, 0)


def shifted_tiles(tile_of, shift_rows, lane):
    steps = jnp.broadcast_to((shift_rows >> 1) + REACH, (ROWS, LANES))
    odd_high = jnp.logical_and(jnp.broadcast_to(shift_rows & 1, (ROWS, LANES)) == 1, lane >= PIX)
    tiles = [tile_of((j + REACH) % TILES) for j in range(TILES)]
    for bit in range(4):
        move = (steps & (1 << bit)) != 0
        tiles = [jnp.where(move, tiles[(j - (1 << bit)) % TILES], tiles[j]) for j in range(TILES)]
    return [jnp.where(odd_high, tiles[j - 1], tiles[j]) for j in range(TILES)]


def offsets_found(a_tile, b_tile, shift_rows, shift_cols):
    lane = lanes_of(ROWS)
    low = lane < PIX
    moved = shifted_tiles(b_tile, shift_rows, lane)
    half = (lane ^ (PIX * (shift_rows & 1))) & PIX
    index = [half | ((lane - shift_cols - e) & (PIX - 1)) for e in (-1, 0, 1)]
    rolled = lambda j: pltpu.roll(a_tile(j % TILES), PIX, 1)
    zero = jnp.zeros((ROWS, LANES), jnp.float32)
    sums = [[zero] * 3 for _ in range(3)]
    energy_a, energy_b = zero, zero
    before, here = rolled(TILES - 1), rolled(0)
    for j in range(TILES):
        after = rolled(j + 1)
        centre = a_tile(j)
        rows_a = (jnp.where(low, before, here), centre, jnp.where(low, here, after))
        cols_b = [pick_rows(moved[j], index[e]) for e in range(3)]
        for e1 in range(3):
            for e2 in range(3):
                sums[e1][e2] = sums[e1][e2] + rows_a[e1] * cols_b[e2]
        energy_a = energy_a + centre * centre
        energy_b = energy_b + cols_b[1] * cols_b[1]
        before, here = here, after
    total = lambda v: jnp.sum(v, axis=1, keepdims=True)
    scale = (total(energy_a) / PIX**2 + 1e-05) * (total(energy_b) / PIX**2 + 1e-05) * PIX**2
    weights = []
    for e1 in range(3):
        corr = [total(sums[e1][e2]) for e2 in range(3)]
        weights.append([c * c / scale for c in corr])
    row_sums = [weights[e][0] + weights[e][1] + weights[e][2] for e in range(3)]
    summed = 1.0 + row_sums[0] + row_sums[1] + row_sums[2]
    col_low = weights[0][0] + weights[1][0] + weights[2][0]
    col_high = weights[0][2] + weights[1][2] + weights[2][2]
    return (
        shift_rows.astype(jnp.float32) + (row_sums[2] - row_sums[0]) / summed,
        shift_cols.astype(jnp.float32) + (col_high - col_low) / summed,
    )


def match_kernel(place, own, partner, prev, shifts, extra, pay):
    first_core = place[0] == 0

    def group(g, row):
        rows = pl.ds(pl.multiple_of(ROWS * g, ROWS), ROWS)
        tile = lambda ref: lambda j: ref[rows, LANES * j : LANES * (j + 1)].astype(jnp.float32)

        def chosen(j):
            at = (rows, slice(LANES * j, LANES * (j + 1)))
            return jnp.where(first_core, own[at].astype(jnp.float32), prev[at].astype(jnp.float32))

        for pair, (a_tile, b_tile) in enumerate(((tile(own), tile(prev)), (tile(partner), chosen))):
            found = offsets_found(
                a_tile, b_tile, shifts[rows, 2 * pair : 2 * pair + 1], shifts[rows, 2 * pair + 1 : 2 * pair + 2]
            )
            for part in range(2):
                at = 32 * (2 * pair + part) + ROWS * g + sublanes_of(ROWS)
                row = row + jnp.where(lanes_of(ROWS) == at, found[part], 0.0)
        return row

    row = lax.fori_loop(0, 2, group, jnp.zeros((ROWS, LANES), jnp.float32))
    pay[...] = extra[...]
    pay[0:1, :] = jnp.sum(row, axis=0, keepdims=True)


def spread_kernel(own, below, above, out):
    lane = lanes_of(1)
    conf = jnp.where(
        lane < 32,
        own[2:3, :],
        jnp.where(
            lane < 64, pltpu.roll(below[2:3, :], 32, 1), jnp.where(lane < 96, pltpu.roll(above[2:3, :], 64, 1), 0.0)
        ),
    )
    rows = [own[0:2, :], below[0:2, :], above[0:2, :], conf, jnp.zeros((1, LANES), jnp.float32)]
    out[...] = jnp.broadcast_to(jnp.concatenate(rows, 0)[None], out.shape)


def relax_kernel(place, gathered, sums_out, fields_out, measured_out, links, left, pushed):
    lane = lanes_of(PLANE)
    sub = sublanes_of(PLANE)

    def assembled(row, quarter):
        total = jnp.zeros((PLANE, LANES), jnp.float32)
        for x in range(4):
            piece = gathered[pl.ds(8 * x + row, PLANE, stride=32), :]
            moved = pltpu.roll(piece, 32 * ((x - quarter) % 4), 1) if x != quarter else piece
            total = jnp.where(lane // 32 == x, moved, total)
        return total

    def window(rows_quarters):
        return jnp.concatenate([assembled(r, q) for r, q in rows_quarters], 0)

    def cores_swapped(values):
        even = sublanes_of(WINDOW) % 2 == 0
        return jnp.where(even, up(values, 1), down(values, 1))

    up = lambda v, k: pltpu.roll(v, v.shape[0] - k, 0)
    down = lambda v, k: pltpu.roll(v, k, 0)

    found = [window([(2, q), (0, q), (4, q)]) for q in range(4)]
    measured = {1: [cores_swapped(found[2]), cores_swapped(found[3])], 2: found[:2]}
    node_links = [window([(3, q), (1, q), (5, q)]).astype(jnp.int32) for q in range(4)]
    confidence = window([(6, 1), (6, 0), (6, 2)])
    section = PLANE * (place[0] - 1) + sublanes_of(WINDOW)
    chain = {d: jnp.where(section >= d, confidence, 0.0) for d, _ in SPRINGS}

    first, last = 4, 18
    node = lax.broadcasted_iota(jnp.int32, (LANES, LANES), 0)
    for s in range(first, last):
        ends = [jnp.where(node == node_links[j][s : s + 1], 1.0, 0.0) for j in range(4)]
        links[s - first] = ((ends[0] + ends[1]) + (ends[2] + ends[3])).astype(jnp.bfloat16)

    def pushed_along(field, begin, end):
        for c in range(2):
            rest = field[c]
            for part in range(3):
                rounded = rest.astype(jnp.bfloat16).astype(jnp.float32)
                left[pl.ds(2 * part + c, WINDOW, stride=8), :] = rounded
                rest = rest - rounded
        for s in range(begin, end):
            pushed[8 * s : 8 * s + 8, :] = lax.dot_general(
                left[8 * s : 8 * s + 8, :].astype(jnp.bfloat16),
                links[s - first],
                (((1,), (1,)), ((), ())),
                preferred_element_type=jnp.float32,
            )
        part = lambda k: pushed[pl.ds(k, WINDOW, stride=8), :]
        return [part(c) + part(2 + c) + part(4 + c) for c in range(2)]

    def image(field, begin, end, degree):
        back = pushed_along(field, begin, end)
        if degree is None:
            degree = pushed[pl.ds(6, WINDOW, stride=8), :]
        out = []
        for c in range(2):
            v = field[c]
            ahead = [pick_rows(v, node_links[j]) for j in range(4)]
            plane = (4.0 + degree) * v - ((ahead[0] + ahead[1]) + (ahead[2] + ahead[3])) - back[c]
            total = plane + ANCHOR * v
            for d, spring in SPRINGS:
                term = chain[d] * (v - down(v, d))
                total = total + spring * (term - up(term, d))
            out.append(total)
        return out, degree

    left[...] = jnp.ones_like(left)
    pushed[...] = jnp.zeros_like(pushed)
    start = []
    for c in range(2):
        total = jnp.zeros((WINDOW, LANES), jnp.float32)
        for d, spring in SPRINGS:
            term = chain[d] * measured[d][c]
            total = total + spring * (up(term, d) - term)
        start.append(total)
    once, degree = image(start, 4, 18, None)
    twice, _ = image(once, 6, 16, degree)

    mid = lambda v: v[PLANE : 2 * PLANE]
    dot = lambda a, b: mid(a[0]) * mid(b[0]) + mid(a[1]) * mid(b[1])
    sums = [dot(start, start), dot(start, once), dot(once, once), dot(once, twice), dot(twice, twice)]
    form = ANCHOR * sums[4]
    for c in range(2):
        v = twice[c]
        for j in range(4):
            differ = mid(v) - pick(mid(v), mid(node_links[j]))
            form = form + differ * differ
        for d, spring in SPRINGS:
            differ = mid(v - down(v, d))
            form = form + spring * mid(chain[d]) * differ * differ
    sums.append(form)
    rows = [jnp.sum(s, axis=0, keepdims=True) for s in sums]
    rows = jnp.concatenate(rows + [jnp.zeros((2, LANES), jnp.float32)], 0)
    totals = jnp.sum(rows, axis=1, keepdims=True)
    line = jnp.sum(jnp.where(lane == sub, totals, 0.0), axis=0, keepdims=True)
    sums_out[...] = jnp.broadcast_to(line[None], sums_out.shape)

    mine = sub == place[1]

    def own(v):
        row = jnp.sum(jnp.where(mine, mid(v), 0.0), axis=0, keepdims=True)
        return pltpu.roll(row, place[2], 1)

    fields = [own(f[c]) for f in (start, once, twice) for c in range(2)]
    fields_out[...] = jnp.concatenate(fields + [jnp.zeros((2, LANES), jnp.float32)], 0)
    for d in (1, 2):
        for c in range(2):
            measured_out[d - 1, c] = own(measured[d][c])[:, :32]


def finish_kernel(sums, fields, out):
    line = jnp.sum(sums[...], axis=0)
    lane = lanes_of(1)
    m = [jnp.sum(jnp.where(lane == k, line, 0.0), axis=1, keepdims=True) for k in range(6)]
    bounded = lambda top, below: jnp.clip(top / below, 0.0, 1.0 / ANCHOR)
    a0 = m[0] / m[1]
    norm = m[0] - 2.0 * a0 * m[1] + a0 * a0 * m[2]
    curve = m[1] - 2.0 * a0 * m[2] + a0 * a0 * m[3]
    a1 = bounded(norm, curve)
    p, q = a0 + a1, a0 * a1
    k1, k2, k3, k4 = -2.0 * p, p * p + 2.0 * q, -2.0 * p * q, q * q
    norm = m[0] + k1 * m[1] + k2 * m[2] + k3 * m[3] + k4 * m[4]
    curve = m[1] + k1 * m[2] + k2 * m[3] + k3 * m[4] + k4 * m[5]
    a2 = bounded(norm, curve)
    for c in range(2):
        v0, v1, v2 = (fields[2 * k + c : 2 * k + c + 1, :] for k in range(3))
        value = (q + a2 * p) * v1 - (p + a2) * v0 - (a2 * q) * v2
        out[c] = value[:, :32]


def on_device(pixels, offsets, connections, confidence):
    z, y, core, x = (lax.axis_index(name) for name in ("z", "y", "core", "x"))
    planes = lax.axis_size("z")
    count = planes * PLANE
    own = pixels[0]
    prev = lax.ppermute(own, SEC, [(i, i + 2) for i in range(count - 2)])
    swap = [(0, 1), (1, 0)]
    partner = lax.ppermute(own, "core", swap)
    partner_offsets = lax.ppermute(offsets[0, :, 0], "core", swap)
    shifts = jnp.concatenate([offsets[1, :, 0], partner_offsets], 0).T
    extra = jnp.zeros((8, LANES), jnp.float32)
    extra = extra.at[1].set(connections.reshape(LANES).astype(jnp.float32))
    extra = extra.at[2, :32].set(confidence[0])
    f32 = jnp.float32

    pay = pl.pallas_call(
        match_kernel,
        out_shape=jax.ShapeDtypeStruct((8, LANES), f32),
        in_specs=[SMEM] + [VMEM] * 5,
        out_specs=VMEM,
        name="match",
    )(core[None].astype(jnp.int32), own, partner, prev, shifts, extra)
    below = lax.ppermute(pay, "z", [(i, i + 1) for i in range(planes - 1)])
    above = lax.ppermute(pay, "z", [(i + 1, i) for i in range(planes - 1)])
    spread = pl.pallas_call(
        spread_kernel,
        out_shape=jax.ShapeDtypeStruct((32, 8, LANES), f32),
        in_specs=[VMEM] * 3,
        out_specs=VMEM,
        name="spread",
    )(pay, below, above)
    gathered = lax.all_to_all(spread, ("y", "core", "x"), 0, 0, tiled=True)
    place = jnp.stack([z, 2 * y + core, (LANES - 32 * x) % LANES]).astype(jnp.int32)
    sums, fields, measured = pl.pallas_call(
        relax_kernel,
        out_shape=(
            jax.ShapeDtypeStruct((planes, 1, LANES), f32),
            jax.ShapeDtypeStruct((8, LANES), f32),
            jax.ShapeDtypeStruct((2, 2, 1, 32), f32),
        ),
        in_specs=[SMEM, VMEM],
        out_specs=(VMEM, VMEM, VMEM),
        scratch_shapes=[
            pltpu.VMEM((14, LANES, LANES), jnp.bfloat16),
            pltpu.VMEM((WINDOW * 8, LANES), f32),
            pltpu.VMEM((WINDOW * 8, LANES), f32),
        ],
        name="relax",
    )(place, gathered.reshape(32 * 8, LANES))
    everywhere = lax.all_to_all(sums, "z", 0, 0, tiled=True)
    displacement = pl.pallas_call(
        finish_kernel,
        out_shape=jax.ShapeDtypeStruct((2, 1, 32), f32),
        in_specs=[VMEM] * 2,
        out_specs=VMEM,
        name="finish",
    )(everywhere, fields)
    return (measured, displacement)


def solution(mesh):
    tiles = mesh.shape["tile"]
    devices = mesh.devices.reshape(mesh.shape["sec"] // PLANE, PLANE // 2, 2, tiles)
    return jax.shard_map(
        on_device,
        mesh=Mesh(devices, ("z", "y", "core", "x")),
        in_specs=(P(SEC, "x", None), P(None, None, SEC, "x"), P(None, SEC, "x"), P(SEC, "x")),
        out_specs=(P(None, None, SEC, "x"), P(None, SEC, "x")),
        check_vma=False,
    )
```

time: 500 us -> 77.9 us (0.16)
  blocking collectives: 346 us -> 26.7 us
  waiting for transfers between devices: 46.3 us -> 11.8 us
  starting transfers between devices: 48 us -> 23.1 us
  between operations: 18.2 us -> 0.77 us
  other arithmetic: 18 us -> 0.63 us
  matrix products: 10.7 us -> 0 us
  Pallas kernels: 0 us -> 9.6 us
  local copies, waits for them, and re-layouts: 10.8 us -> 4.83 us
    psum x3 -> x0, blocking collectives: 319 us -> none  [on_device(): grad_sq = lax.psum(jnp.sum(gradient * gradient), ('sec', 'tile'))]
    unnamed x6 -> x0, waiting for transfers between devices: 42.8 us -> none
    ppermute x16 -> x5, starting transfers between devices: 47.9 us -> 16.1 us  [the longest x1 8.79 us: on_device(): partner = lax.ppermute(own, 'core', swap)]
    all_gather x3 -> x0, blocking collectives: 27.2 us -> none  [on_device(): gathered = lax.all_gather(gradient, 'tile', axis=2, tiled=True)]
    all_to_all x0 -> x1, blocking collectives: none -> 26.7 us  [on_device(): everywhere = lax.all_to_all(sums, 'z', 0, 0, tiled=True)]
    dot_general x12 -> x0, matrix products: 10.7 us -> none  [the longest x2 3.83 us: patch_scores(): jnp.einsum('bkc,bgc->bkg', cross, phase_table, precision=lax.Precision.HI...]
    pallas_call x0 -> x4, Pallas kernels: none -> 9.6 us  [the longest x1 3.97 us: on_device(): pl.pallas_call(match_kernel, out_shape=jax.ShapeDtypeStruct((8, LANES), f...]
    all_to_all x0 -> x1, starting transfers between devices: none -> 7.01 us  [on_device(): gathered = lax.all_to_all(spread, ('y', 'core', 'x'), 0, 0, tiled=True)]
  transfers between devices with their start and end apart: 19 -> 6, of which waited for: 4 -> 3; matrix products, arithmetic and copies ran while one was open for 3% -> 3% of each run, Pallas kernels for 0% -> 0%
where the time goes in v1:
time: 77.9 us; the launch traced here: 77.4 us
  blocking collectives  26.7 us (34%)
  starting transfers between devices  23.1 us (30%)
  waiting for transfers between devices  11.8 us (15%)
  Pallas kernels  9.6 us (12%)
  local copies, waits for them, and re-layouts  4.83 us (6%)
    all_to_all x1, blocking collectives, on_device(): everywhere = lax.all_to_all(sums, 'z', 0, 0, tiled=True)  26.7 us
    ppermute x1, starting transfers between devices, on_device(): partner = lax.ppermute(own, 'core', swap)  8.79 us
    all_to_all x1, starting transfers between devices, on_device(): gathered = lax.all_to_all(spread, ('y', 'core', 'x'), 0, 0, tiled=True)  7.01 us
    all_to_all x1, waiting for transfers between devices, on_device(): gathered = lax.all_to_all(spread, ('y', 'core', 'x'), 0, 0, tiled=True)  7 us
    pallas_call x1, Pallas kernels, on_device(): pl.pallas_call(match_kernel, out_shape=jax.ShapeDtypeStruct((8, LANES), f...  3.97 us
    ppermute x1, waiting for transfers between devices, on_device(): above = lax.ppermute(pay, 'z', [(i + 1, i) for i in range(planes - 1)])  3.43 us
    unnamed x16, local copies, waits for them, and re-layouts  3.27 us
    pallas_call x1, Pallas kernels, on_device(): pl.pallas_call(relax_kernel, out_shape=(jax.ShapeDtypeStruct((planes, 1,...  2.82 us
  transfers between devices with their start and end apart: 6, of which 3 were waited for; matrix products, arithmetic and copies ran while one was open for 3% of the time, Pallas kernels for 0%

profile of v1, /device:TPU:1, one launch (start us, length us, event | category | flops | bytes accessed | tf_op | source)
XLA Modules:
  0.0 77.4 jit_solution(6167558852722734631)
XLA Ops:
  0.6 8.8 %collective-permute-start = (bf16[32,4096]{1,0:T(8,128)(2,1)}, bf16[32,4096]{1,0:T(8,128)(2,1)S(1)}, u32[]{:S(2)}, u32[]{:S(2)}) collective-permute-start(bf16[32,4096]{1,0:T(8,128)(2,1)} %bitcast.10), channel_id=1, source_target_pairs={{0,4},{4,0},{1,5},{5,1},{2,6},{6,2},{3,7},{7,3},{8,12},{12,8},{9,1... | collective-permute-start | bytes 786440 | tf_op jit(solution)/shard_map/ppermute | solution.py:265
  9.4 1.3 %collective-permute-start.1 = (bf16[32,4096]{1,0:T(8,128)(2,1)}, bf16[32,4096]{1,0:T(8,128)(2,1)S(1)}, u32[]{:S(2)}, u32[]{:S(2)}) collective-permute-start(bf16[32,4096]{1,0:T(8,128)(2,1)} %bitcast.11), channel_id=1, source_target_pairs={{0,8},{4,12},{8,16},{12,20},{16,24},{20,28},{24,32},{28,36},{32,40... | collective-permute-start | bytes 786440 | tf_op jit(solution)/shard_map/ppermute | solution.py:263
  10.7 0.7 fusion
  11.4 1.9 %collective-permute-start.2 = (s32[2,32]{1,0:T(2,128)S(1)}, s32[2,32]{1,0:T(2,128)S(1)}, u32[]{:S(2)}, u32[]{:S(2)}) collective-permute-start(s32[2,32]{1,0:T(2,128)S(1)} %bitcast.15), channel_id=1, source_target_pairs={{0,4},{4,0},{1,5},{5,1},{2,6},{6,2},{3,7},{7,3},{8,12},{12,8},{9,1... | collective-permute-start | bytes 776 | tf_op jit(solution)/shard_map/ppermute | solution.py:266
  13.4 0.0 copy-start.6
  13.4 0.7 copy-done.6
  14.1 0.1 convert_element_type.12
  14.2 0.0 copy-start.7
  14.2 0.6 copy-done.7
  14.8 0.1 scatter.9.extra
  14.9 0.0 copy-start.3
  14.9 0.0 collective-permute-done.2
  14.9 0.7 copy.8
  15.6 0.0 copy-done.3
  15.6 0.0 collective-permute-done.partner
  15.6 0.0 copy-start.1
  15.6 1.3 %collective-permute-done.1.prev = bf16[32,4096]{1,0:T(8,128)(2,1)S(1)} collective-permute-done((bf16[32,4096]{1,0:T(8,128)(2,1)}, bf16[32,4096]{1,0:T(8,128)(2,1)S(1)}, u32[]{:S(2)}, u32[]{:S(2)}) %collective-permute-start.1) | collective-permute-done | bytes 262176 | tf_op jit(solution)/shard_map/ppermute | solution.py:263
  17.0 0.0 copy-start.2
  17.0 0.0 copy-done.1
  17.0 0.7 copy-done.2
  17.7 4.0 %match.1.own = f32[8,128]{1,0:T(8,128)} custom-call(s32[1]{0:T(128)} %bitcast.3.place, bf16[32,4096]{1,0:T(8,128)(2,1)} %bitcast.12, bf16[32,4096]{1,0:T(8,128)(2,1)} %copy-done.1, bf16[32,4096]{1,0:T(8,128)(2,1)} %copy-done.2, s32[32,4]{1,0:T(8,128)} %bitcast.13, f32[8,128]{1,0:T(8,128)} %copy-done.3), custom_call_target="tpu_custom_call" | custom-call | tf_op jit(solution)/shard_map/match/pallas_call | solution.py:273
  21.6 2.8 %collective-permute-start.3 = (f32[8,128]{1,0:T(8,128)}, f32[8,128]{1,0:T(8,128)S(1)}, u32[]{:S(2)}, u32[]{:S(2)}) collective-permute-start(f32[8,128]{1,0:T(8,128)} %match.1.own), channel_id=1, source_target_pairs={{0,32},{32,64},{64,96},{96,128},{128,160},{160,192},{192,224},{224... | collective-permute-start | bytes 12296 | tf_op jit(solution)/shard_map/ppermute | solution.py:280
  24.4 1.3 %collective-permute-start.4 = (f32[8,128]{1,0:T(8,128)}, f32[8,128]{1,0:T(8,128)S(1)}, u32[]{:S(2)}, u32[]{:S(2)}) collective-permute-start(f32[8,128]{1,0:T(8,128)} %match.1.own), channel_id=1, source_target_pairs={{32,0},{64,32},{96,64},{128,96},{160,128},{192,160},{224,192},{256... | collective-permute-start | bytes 12296 | tf_op jit(solution)/shard_map/ppermute | solution.py:281
  25.7 0.0 collective-permute-done.3.below
  25.7 0.0 copy-start.4
  25.7 3.4 %collective-permute-done.4.above = f32[8,128]{1,0:T(8,128)S(1)} collective-permute-done((f32[8,128]{1,0:T(8,128)}, f32[8,128]{1,0:T(8,128)S(1)}, u32[]{:S(2)}, u32[]{:S(2)}) %collective-permute-start.4) | collective-permute-done | bytes 4128 | tf_op jit(solution)/shard_map/ppermute | solution.py:281
  29.2 0.0 copy-done.4
  29.2 0.0 copy-start.5
  29.2 0.6 copy-done.5
  29.7 1.4 %spread.1 = f32[32,8,128]{2,1,0:T(8,128)} custom-call(f32[8,128]{1,0:T(8,128)} %match.1.own, f32[8,128]{1,0:T(8,128)} %copy-done.4, f32[8,128]{1,0:T(8,128)} %copy-done.5), custom_call_target="tpu_custom_call" | custom-call | tf_op jit(solution)/shard_map/spread/pallas_call | solution.py:282
  31.2 7.0 %all-to-all-start = ((f32[32,8,128]{2,1,0:T(8,128)}), f32[32,8,128]{2,1,0:T(8,128)S(1)}, u32[]{:S(2)}, u32[]{:S(2)}) async-start(f32[32,8,128]{2,1,0:T(8,128)} %spread.1), calls=%async_computation | async-start | bytes 262144 | tf_op jit(solution)/shard_map/all_to_all | solution.py:289
  38.2 0.6 pad_add_fusion.1.place
  38.8 7.0 %all-to-all-done = f32[32,8,128]{2,1,0:T(8,128)S(1)} async-done(((f32[32,8,128]{2,1,0:T(8,128)}), f32[32,8,128]{2,1,0:T(8,128)S(1)}, u32[]{:S(2)}, u32[]{:S(2)}) %all-to-all-start) | async-done | bytes 131104 | tf_op jit(solution)/shard_map/all_to_all | solution.py:289
  45.8 0.0 copy-start
  45.8 0.6 copy-done
  46.5 2.8 %relax.1 = (f32[16,1,128]{2,1,0:T(1,128)}, f32[8,128]{1,0:T(8,128)}, f32[2,2,1,32]{3,2,1,0:T(1,128)}) custom-call(s32[3]{0:T(128)} %pad_add_fusion.1.place, f32[256,128]{1,0:T(8,128)} %bitcast.9), custom_call_target="tpu_custom_call" | custom-call | tf_op jit(solution)/shard_map/relax/pallas_call | solution.py:291
  49.3 26.7 %all_to_all.10.sums = f32[16,1,128]{2,1,0:T(1,128)} all-to-all(f32[16,1,128]{2,1,0:T(1,128)} %get-tuple-element.30), channel_id=1, replica_groups=mesh['z'=16,'y'=4,'core'=2,'x'=4] {'z'}, dimensions={0} | all-to-all | bytes 16384 | tf_op jit(solution)/shard_map/all_to_all | solution.py:307
  76.0 1.4 %finish.1 = f32[2,1,32]{2,1,0:T(1,128)} custom-call(f32[16,1,128]{2,1,0:T(1,128)} %all_to_all.10.sums, f32[8,128]{1,0:T(8,128)} %get-tuple-element.31.fields), custom_call_target="tpu_custom_call" | custom-call | tf_op jit(solution)/shard_map/finish/pallas_call | solution.py:308
  (3 shorter events, 0.0 us)
Async XLA Ops:
  0.6 15.0 %collective-permute-start = (bf16[32,4096]{1,0:T(8,128)(2,1)}, bf16[32,4096]{1,0:T(8,128)(2,1)S(1)}, u32[]{:S(2)}, u32[]{:S(2)}) collective-permute-start(bf16[32,4096]{1,0:T(8,128)(2,1)} %bitcast.10), channel_id=1, source_target_pairs={{0,4},{4,0},{1,5},{5,1},{2,6},{6,2},{3,7},{7,3},{8,12},{12,8},{9,1... | collective-permute-start | bytes 786440 | tf_op jit(solution)/shard_map/ppermute | solution.py:265
  9.4 7.5 %collective-permute-start.1 = (bf16[32,4096]{1,0:T(8,128)(2,1)}, bf16[32,4096]{1,0:T(8,128)(2,1)S(1)}, u32[]{:S(2)}, u32[]{:S(2)}) collective-permute-start(bf16[32,4096]{1,0:T(8,128)(2,1)} %bitcast.11), channel_id=1, source_target_pairs={{0,8},{4,12},{8,16},{12,20},{16,24},{20,28},{24,32},{28,36},{32,40... | collective-permute-start | bytes 786440 | tf_op jit(solution)/shard_map/ppermute | solution.py:263
  11.4 3.5 %collective-permute-start.2 = (s32[2,32]{1,0:T(2,128)S(1)}, s32[2,32]{1,0:T(2,128)S(1)}, u32[]{:S(2)}, u32[]{:S(2)}) collective-permute-start(s32[2,32]{1,0:T(2,128)S(1)} %bitcast.15), channel_id=1, source_target_pairs={{0,4},{4,0},{1,5},{5,1},{2,6},{6,2},{3,7},{7,3},{8,12},{12,8},{9,1... | collective-permute-start | bytes 776 | tf_op jit(solution)/shard_map/ppermute | solution.py:266
  13.4 0.7 copy-start.6
  14.2 0.7 copy-start.7
  14.9 0.7 copy-start.3
  15.6 1.3 %copy-start.1 = (bf16[32,4096]{1,0:T(8,128)(2,1)}, bf16[32,4096]{1,0:T(8,128)(2,1)S(1)}, u32[]{:S(2)}) copy-start(bf16[32,4096]{1,0:T(8,128)(2,1)S(1)} %collective-permute-done.partner) | copy-start | bytes 786436
  17.0 0.7 copy-start.2
  21.6 4.1 %collective-permute-start.3 = (f32[8,128]{1,0:T(8,128)}, f32[8,128]{1,0:T(8,128)S(1)}, u32[]{:S(2)}, u32[]{:S(2)}) collective-permute-start(f32[8,128]{1,0:T(8,128)} %match.1.own), channel_id=1, source_target_pairs={{0,32},{32,64},{64,96},{96,128},{128,160},{160,192},{192,224},{224... | collective-permute-start | bytes 12296 | tf_op jit(solution)/shard_map/ppermute | solution.py:280
  24.4 4.7 %collective-permute-start.4 = (f32[8,128]{1,0:T(8,128)}, f32[8,128]{1,0:T(8,128)S(1)}, u32[]{:S(2)}, u32[]{:S(2)}) collective-permute-start(f32[8,128]{1,0:T(8,128)} %match.1.own), channel_id=1, source_target_pairs={{32,0},{64,32},{96,64},{128,96},{160,128},{192,160},{224,192},{256... | collective-permute-start | bytes 12296 | tf_op jit(solution)/shard_map/ppermute | solution.py:281
  25.7 3.4 %copy-start.4 = (f32[8,128]{1,0:T(8,128)}, f32[8,128]{1,0:T(8,128)S(1)}, u32[]{:S(2)}) copy-start(f32[8,128]{1,0:T(8,128)S(1)} %collective-permute-done.3.below) | copy-start | bytes 12292
  29.2 0.6 copy-start.5
  31.2 14.6 %all-to-all-start = ((f32[32,8,128]{2,1,0:T(8,128)}), f32[32,8,128]{2,1,0:T(8,128)S(1)}, u32[]{:S(2)}, u32[]{:S(2)}) async-start(f32[32,8,128]{2,1,0:T(8,128)} %spread.1), calls=%async_computation | async-start | bytes 262144 | tf_op jit(solution)/shard_map/all_to_all | solution.py:289
  45.8 0.7 copy-start

commit v2 on v1

--- a/solution.py
+++ b/solution.py
@@ -18,6 +18,10 @@
 SEC = ("z", "y", "core")
 VMEM = pl.BlockSpec(memory_space=pltpu.VMEM)
 SMEM = pl.BlockSpec(memory_space=pltpu.SMEM)
+
+
+def kept(array):
+    return pltpu.with_memory_space_constraint(array, pltpu.VMEM)
 
 
 def lanes_of(rows):
@@ -272,27 +276,27 @@
 
     pay = pl.pallas_call(
         match_kernel,
-        out_shape=jax.ShapeDtypeStruct((8, LANES), f32),
+        out_shape=pltpu.VMEM((8, LANES), f32),
         in_specs=[SMEM] + [VMEM] * 5,
         out_specs=VMEM,
         name="match",
-    )(core[None].astype(jnp.int32), own, partner, prev, shifts, extra)
+    )(core[None].astype(jnp.int32), *[kept(v) for v in (own, partner, prev, shifts, extra)])
     below = lax.ppermute(pay, "z", [(i, i + 1) for i in range(planes - 1)])
     above = lax.ppermute(pay, "z", [(i + 1, i) for i in range(planes - 1)])
     spread = pl.pallas_call(
         spread_kernel,
-        out_shape=jax.ShapeDtypeStruct((32, 8, LANES), f32),
+        out_shape=pltpu.VMEM((32, 8, LANES), f32),
         in_specs=[VMEM] * 3,
         out_specs=VMEM,
         name="spread",
-    )(pay, below, above)
+    )(kept(pay), kept(below), kept(above))
     gathered = lax.all_to_all(spread, ("y", "core", "x"), 0, 0, tiled=True)
     place = jnp.stack([z, 2 * y + core, (LANES - 32 * x) % LANES]).astype(jnp.int32)
     sums, fields, measured = pl.pallas_call(
         relax_kernel,
         out_shape=(
-            jax.ShapeDtypeStruct((planes, 1, LANES), f32),
-            jax.ShapeDtypeStruct((8, LANES), f32),
+            pltpu.VMEM((planes, 1, LANES), f32),
+            pltpu.VMEM((8, LANES), f32),
             jax.ShapeDtypeStruct((2, 2, 1, 32), f32),
         ),
         in_specs=[SMEM, VMEM],
@@ -303,15 +307,16 @@
             pltpu.VMEM((WINDOW * 8, LANES), f32),
         ],
         name="relax",
-    )(place, gathered.reshape(32 * 8, LANES))
-    everywhere = lax.all_to_all(sums, "z", 0, 0, tiled=True)
+    )(place, kept(gathered.reshape(32 * 8, LANES)))
+    turned = [[(i + planes // 2) % planes for i in range(planes)]]
+    everywhere = lax.all_to_all(sums, "z", 0, 0, tiled=True, axis_index_groups=turned)
     displacement = pl.pallas_call(
         finish_kernel,
         out_shape=jax.ShapeDtypeStruct((2, 1, 32), f32),
         in_specs=[VMEM] * 2,
         out_specs=VMEM,
         name="finish",
-    )(everywhere, fields)
+    )(kept(everywhere), kept(fields))
     return (measured, displacement)
 
 

time: 77.9 us -> 65.6 us (0.84)
  blocking collectives: 26.7 us -> 19.1 us
  Pallas kernels: 9.6 us -> 6.22 us
  local copies, waits for them, and re-layouts: 4.83 us -> 3.24 us
    all_to_all x1, blocking collectives: 26.7 us -> 19.1 us  [on_device(): lax.all_to_all(sums, 'z', 0, 0, tiled=True, axis_index_groups=turned)]
    pallas_call x3, Pallas kernels: 8.2 us -> 5.52 us  [the longest x1 2.54 us: on_device(): pl.pallas_call(relax_kernel, out_shape=(pltpu.VMEM((planes, 1, LANES), f3...]
    unnamed x16 -> x6, local copies, waits for them, and re-layouts: 3.27 us -> 2.27 us
  transfers between devices with their start and end apart: 6 -> 6, of which waited for: 3 -> 3; matrix products, arithmetic and copies ran while one was open for 3% -> 2% of each run, Pallas kernels for 0% -> 0%
where the time goes in v2:
time: 65.6 us; the launch traced here: 65.2 us
  starting transfers between devices  23.1 us (35%)
  blocking collectives  19.1 us (29%)
  waiting for transfers between devices  12.2 us (19%)
  Pallas kernels  6.22 us (9%)
  local copies, waits for them, and re-layouts  3.24 us (5%)
  between operations  0.75 us (1%)
    all_to_all x1, blocking collectives, on_device(): lax.all_to_all(sums, 'z', 0, 0, tiled=True, axis_index_groups=turned)  19.1 us
    ppermute x1, starting transfers between devices, on_device(): partner = lax.ppermute(own, 'core', swap)  8.79 us
    all_to_all x1, waiting for transfers between devices, on_device(): gathered = lax.all_to_all(spread, ('y', 'core', 'x'), 0, 0, tiled=True)  7.04 us
    all_to_all x1, starting transfers between devices, on_device(): gathered = lax.all_to_all(spread, ('y', 'core', 'x'), 0, 0, tiled=True)  7.01 us
    ppermute x1, waiting for transfers between devices, on_device(): above = lax.ppermute(pay, 'z', [(i + 1, i) for i in range(planes - 1)])  3.23 us
    ppermute x1, starting transfers between devices, on_device(): below = lax.ppermute(pay, 'z', [(i, i + 1) for i in range(planes - 1)])  2.78 us
    pallas_call x1, Pallas kernels, on_device(): pl.pallas_call(relax_kernel, out_shape=(pltpu.VMEM((planes, 1, LANES), f3...  2.54 us
    unnamed x6, local copies, waits for them, and re-layouts  2.27 us
  transfers between devices with their start and end apart: 6, of which 3 were waited for; matrix products, arithmetic and copies ran while one was open for 2% of the time, Pallas kernels for 0%

profile of v2, /device:TPU:1, one launch (start us, length us, event | category | flops | bytes accessed | tf_op | source)
XLA Modules:
  0.0 65.2 jit_solution(9544501025169145369)
XLA Ops:
  0.6 8.8 %collective-permute-start = (bf16[32,4096]{1,0:T(8,128)(2,1)}, bf16[32,4096]{1,0:T(8,128)(2,1)S(1)}, u32[]{:S(2)}, u32[]{:S(2)}) collective-permute-start(bf16[32,4096]{1,0:T(8,128)(2,1)} %bitcast.10), channel_id=1, source_target_pairs={{0,4},{4,0},{1,5},{5,1},{2,6},{6,2},{3,7},{7,3},{8,12},{12,8},{9,1... | collective-permute-start | bytes 786440 | tf_op jit(solution)/shard_map/ppermute | solution.py:269
  9.4 1.3 %collective-permute-start.1 = (bf16[32,4096]{1,0:T(8,128)(2,1)}, bf16[32,4096]{1,0:T(8,128)(2,1)S(1)}, u32[]{:S(2)}, u32[]{:S(2)}) collective-permute-start(bf16[32,4096]{1,0:T(8,128)(2,1)} %bitcast.11), channel_id=1, source_target_pairs={{0,8},{4,12},{8,16},{12,20},{16,24},{20,28},{24,32},{28,36},{32,40... | collective-permute-start | bytes 786440 | tf_op jit(solution)/shard_map/ppermute | solution.py:267
  10.7 0.7 %fusion = (s32[1,2,1,32]{3,2,1,0:T(1,128)S(1)}, s32[1,2,1,32]{3,2,1,0:T(1,128)S(1)}) fusion(s32[2,2,1,32]{3,2,1,0:T(1,128)} %param.9), kind=kLoop, calls=%fused_computation.3 | loop fusion | bytes 1024 | tf_op jit(solution)/shard_map/slice | solution.py:271
  11.4 1.9 %collective-permute-start.2 = (s32[2,32]{1,0:T(2,128)S(1)}, s32[2,32]{1,0:T(2,128)S(1)}, u32[]{:S(2)}, u32[]{:S(2)}) collective-permute-start(s32[2,32]{1,0:T(2,128)S(1)} %bitcast.15), channel_id=1, source_target_pairs={{0,4},{4,0},{1,5},{5,1},{2,6},{6,2},{3,7},{7,3},{8,12},{12,8},{9,1... | collective-permute-start | bytes 776 | tf_op jit(solution)/shard_map/ppermute | solution.py:270
  13.4 0.0 copy-start.1
  13.4 0.7 %copy-done.1 = s32[4,1,32]{2,1,0:T(1,128)S(1)} copy-done((s32[4,1,32]{2,1,0:T(1,128)S(1)}, s32[4,1,32]{2,1,0:T(1,128)}, u32[]{:S(2)}) %copy-start.1) | copy-done | bytes 536
  14.1 0.1 convert_element_type.12
  14.2 0.0 copy-start.2
  14.2 0.6 copy-done.2
  14.8 0.1 scatter.9.extra
  14.9 0.0 collective-permute-done.2
  14.9 0.1 copy.8
  15.0 0.0 collective-permute-done.partner
  15.0 1.9 %collective-permute-done.1.prev = bf16[32,4096]{1,0:T(8,128)(2,1)S(1)} collective-permute-done((bf16[32,4096]{1,0:T(8,128)(2,1)}, bf16[32,4096]{1,0:T(8,128)(2,1)S(1)}, u32[]{:S(2)}, u32[]{:S(2)}) %collective-permute-start.1) | collective-permute-done | bytes 262176 | tf_op jit(solution)/shard_map/ppermute | solution.py:267
  17.0 0.0 copy-start
  17.0 0.9 %copy-done = bf16[1,32,4096]{2,1,0:T(8,128)(2,1)S(1)} copy-done((bf16[1,32,4096]{2,1,0:T(8,128)(2,1)S(1)}, bf16[1,32,4096]{2,1,0:T(8,128)(2,1)}, u32[]{:S(2)}) %copy-start) | copy-done | bytes 262168
  17.9 2.3 %match.1.own = f32[8,128]{1,0:T(8,128)S(1)} custom-call(s32[1]{0:T(128)} %bitcast.3.place, bf16[32,4096]{1,0:T(8,128)(2,1)S(1)} %bitcast.12, bf16[32,4096]{1,0:T(8,128)(2,1)S(1)} %collective-permute-done.partner, bf16[32,4096]{1,0:T(8,128)(2,1)S(1)} %collective-permute-done.1.prev, s32[32,4]{1,0:T(8,128)S(1)} %bitcast.13, f32[8,128]{1,0:T(8,128)S(1)} %scatter.9.extra), custom_call_target="tpu_custom_call" | custom-call | tf_op jit(solution)/shard_map/match/pallas_call | solution.py:277
  20.2 2.8 %collective-permute-start.3 = (f32[8,128]{1,0:T(8,128)S(1)}, f32[8,128]{1,0:T(8,128)S(1)}, u32[]{:S(2)}, u32[]{:S(2)}) collective-permute-start(f32[8,128]{1,0:T(8,128)S(1)} %match.1.own), channel_id=1, source_target_pairs={{0,32},{32,64},{64,96},{96,128},{128,160},{160,192},{192,224},{224... | collective-permute-start | bytes 12296 | tf_op jit(solution)/shard_map/ppermute | solution.py:284
  23.0 1.3 %collective-permute-start.4 = (f32[8,128]{1,0:T(8,128)S(1)}, f32[8,128]{1,0:T(8,128)S(1)}, u32[]{:S(2)}, u32[]{:S(2)}) collective-permute-start(f32[8,128]{1,0:T(8,128)S(1)} %match.1.own), channel_id=1, source_target_pairs={{32,0},{64,32},{96,64},{128,96},{160,128},{192,160},{224,192},{256... | collective-permute-start | bytes 12296 | tf_op jit(solution)/shard_map/ppermute | solution.py:285
  24.3 0.0 collective-permute-done.3.below
  24.3 3.2 %collective-permute-done.4.above = f32[8,128]{1,0:T(8,128)S(1)} collective-permute-done((f32[8,128]{1,0:T(8,128)S(1)}, f32[8,128]{1,0:T(8,128)S(1)}, u32[]{:S(2)}, u32[]{:S(2)}) %collective-permute-start.4) | collective-permute-done | bytes 4128 | tf_op jit(solution)/shard_map/ppermute | solution.py:285
  27.5 0.7 %spread.1 = f32[32,8,128]{2,1,0:T(8,128)} custom-call(f32[8,128]{1,0:T(8,128)S(1)} %match.1.own, f32[8,128]{1,0:T(8,128)S(1)} %collective-permute-done.3.below, f32[8,128]{1,0:T(8,128)S(1)} %collective-permute-done.4.above), custom_call_target="tpu_custom_call" | custom-call | tf_op jit(solution)/shard_map/spread/pallas_call | solution.py:286
  28.2 7.0 %all-to-all-start = ((f32[32,8,128]{2,1,0:T(8,128)}), f32[32,8,128]{2,1,0:T(8,128)S(1)}, u32[]{:S(2)}, u32[]{:S(2)}) async-start(f32[32,8,128]{2,1,0:T(8,128)} %spread.1), calls=%async_computation | async-start | bytes 262144 | tf_op jit(solution)/shard_map/all_to_all | solution.py:293
  35.3 0.6 pad_add_fusion.1.place
  35.8 7.0 %all-to-all-done = f32[32,8,128]{2,1,0:T(8,128)S(1)} async-done(((f32[32,8,128]{2,1,0:T(8,128)}), f32[32,8,128]{2,1,0:T(8,128)S(1)}, u32[]{:S(2)}, u32[]{:S(2)}) %all-to-all-start) | async-done | bytes 131104 | tf_op jit(solution)/shard_map/all_to_all | solution.py:293
  42.9 2.5 %relax.1 = (f32[16,1,128]{2,1,0:T(1,128)S(1)}, f32[8,128]{1,0:T(8,128)S(1)}, f32[2,2,1,32]{3,2,1,0:T(1,128)}) custom-call(s32[3]{0:T(128)} %pad_add_fusion.1.place, f32[256,128]{1,0:T(8,128)S(1)} %bitcast.9), custom_call_target="tpu_custom_call" | custom-call | tf_op jit(solution)/shard_map/relax/pallas_call | solution.py:295
  45.4 19.1 %all_to_all.10.sums = f32[16,1,128]{2,1,0:T(1,128)S(1)} all-to-all(f32[16,1,128]{2,1,0:T(1,128)S(1)} %get-tuple-element.30), channel_id=1, replica_groups={{256,288,320,352,384,416,448,480,0,32,64,96,128,160,192,224},{257,289,3..., dimensions={0} | all-to-all | bytes 16384 | tf_op jit(solution)/shard_map/all_to_all | solution.py:312
  64.5 0.7 %finish.1 = f32[2,1,32]{2,1,0:T(1,128)} custom-call(f32[16,1,128]{2,1,0:T(1,128)S(1)} %all_to_all.10.sums, f32[8,128]{1,0:T(8,128)S(1)} %get-tuple-element.31.fields), custom_call_target="tpu_custom_call" | custom-call | tf_op jit(solution)/shard_map/finish/pallas_call | solution.py:313
  (3 shorter events, 0.0 us)
Async XLA Ops:
  0.6 14.4 %collective-permute-start = (bf16[32,4096]{1,0:T(8,128)(2,1)}, bf16[32,4096]{1,0:T(8,128)(2,1)S(1)}, u32[]{:S(2)}, u32[]{:S(2)}) collective-permute-start(bf16[32,4096]{1,0:T(8,128)(2,1)} %bitcast.10), channel_id=1, source_target_pairs={{0,4},{4,0},{1,5},{5,1},{2,6},{6,2},{3,7},{7,3},{8,12},{12,8},{9,1... | collective-permute-start | bytes 786440 | tf_op jit(solution)/shard_map/ppermute | solution.py:269
  9.4 7.5 %collective-permute-start.1 = (bf16[32,4096]{1,0:T(8,128)(2,1)}, bf16[32,4096]{1,0:T(8,128)(2,1)S(1)}, u32[]{:S(2)}, u32[]{:S(2)}) collective-permute-start(bf16[32,4096]{1,0:T(8,128)(2,1)} %bitcast.11), channel_id=1, source_target_pairs={{0,8},{4,12},{8,16},{12,20},{16,24},{20,28},{24,32},{28,36},{32,40... | collective-permute-start | bytes 786440 | tf_op jit(solution)/shard_map/ppermute | solution.py:267
  11.4 3.5 %collective-permute-start.2 = (s32[2,32]{1,0:T(2,128)S(1)}, s32[2,32]{1,0:T(2,128)S(1)}, u32[]{:S(2)}, u32[]{:S(2)}) collective-permute-start(s32[2,32]{1,0:T(2,128)S(1)} %bitcast.15), channel_id=1, source_target_pairs={{0,4},{4,0},{1,5},{5,1},{2,6},{6,2},{3,7},{7,3},{8,12},{12,8},{9,1... | collective-permute-start | bytes 776 | tf_op jit(solution)/shard_map/ppermute | solution.py:270
  13.4 0.7 %copy-start.1 = (s32[4,1,32]{2,1,0:T(1,128)S(1)}, s32[4,1,32]{2,1,0:T(1,128)}, u32[]{:S(2)}) copy-start(s32[4,1,32]{2,1,0:T(1,128)} %param.10) | copy-start | bytes 1540
  14.2 0.7 %copy-start.2 = (f32[1,32]{1,0:T(1,128)S(1)}, f32[1,32]{1,0:T(1,128)}, u32[]{:S(2)}) copy-start(f32[1,32]{1,0:T(1,128)} %param.11) | copy-start | bytes 388
  17.0 0.9 %copy-start = (bf16[1,32,4096]{2,1,0:T(8,128)(2,1)S(1)}, bf16[1,32,4096]{2,1,0:T(8,128)(2,1)}, u32[]{:S(2)}) copy-start(bf16[1,32,4096]{2,1,0:T(8,128)(2,1)} %param.8) | copy-start | bytes 786436
  20.2 4.1 %collective-permute-start.3 = (f32[8,128]{1,0:T(8,128)S(1)}, f32[8,128]{1,0:T(8,128)S(1)}, u32[]{:S(2)}, u32[]{:S(2)}) collective-permute-start(f32[8,128]{1,0:T(8,128)S(1)} %match.1.own), channel_id=1, source_target_pairs={{0,32},{32,64},{64,96},{96,128},{128,160},{160,192},{192,224},{224... | collective-permute-start | bytes 12296 | tf_op jit(solution)/shard_map/ppermute | solution.py:284
  23.0 4.5 %collective-permute-start.4 = (f32[8,128]{1,0:T(8,128)S(1)}, f32[8,128]{1,0:T(8,128)S(1)}, u32[]{:S(2)}, u32[]{:S(2)}) collective-permute-start(f32[8,128]{1,0:T(8,128)S(1)} %match.1.own), channel_id=1, source_target_pairs={{32,0},{64,32},{96,64},{128,96},{160,128},{192,160},{224,192},{256... | collective-permute-start | bytes 12296 | tf_op jit(solution)/shard_map/ppermute | solution.py:285
  28.2 14.6 %all-to-all-start = ((f32[32,8,128]{2,1,0:T(8,128)}), f32[32,8,128]{2,1,0:T(8,128)S(1)}, u32[]{:S(2)}, u32[]{:S(2)}) async-start(f32[32,8,128]{2,1,0:T(8,128)} %spread.1), calls=%async_computation | async-start | bytes 262144 | tf_op jit(solution)/shard_map/all_to_all | solution.py:293

commit v3 on v2

--- a/solution.py
+++ b/solution.py
@@ -89,8 +89,26 @@
     )
 
 
-def match_kernel(place, own, partner, prev, shifts, extra, pay):
-    first_core = place[0] == 0
+def prep_kernel(pixels, offsets, connections, confidence, own, shifts, extra):
+    own[...] = pixels[...]
+    rows = sublanes_of(ROWS)
+    lane = lanes_of(ROWS)
+    for g in range(2):
+        tile = jnp.zeros((ROWS, LANES), jnp.float32)
+        for d in range(2):
+            for part in range(2):
+                row = offsets[d, part].astype(jnp.float32)
+                chosen = jnp.where(lane[:, :32] == rows[:, :32] + ROWS * g, row, 0.0)
+                tile = jnp.where(lane == 2 * d + part, jnp.sum(chosen, axis=1, keepdims=True), tile)
+        shifts[ROWS * g : ROWS * (g + 1), :] = tile
+    extra[...] = jnp.zeros_like(extra)
+    for j in range(4):
+        extra[1:2, 32 * j : 32 * (j + 1)] = connections[j].astype(jnp.float32)
+    extra[2:3, 0:32] = confidence[...]
+
+
+def match_kernel(place, own, partner, prev, own_offsets, partner_offsets, extra, pay):
+    first_core = place[3] == 0
 
     def group(g, row):
         rows = pl.ds(pl.multiple_of(ROWS * g, ROWS), ROWS)
@@ -100,10 +118,11 @@
             at = (rows, slice(LANES * j, LANES * (j + 1)))
             return jnp.where(first_core, own[at].astype(jnp.float32), prev[at].astype(jnp.float32))
 
-        for pair, (a_tile, b_tile) in enumerate(((tile(own), tile(prev)), (tile(partner), chosen))):
-            found = offsets_found(
-                a_tile, b_tile, shifts[rows, 2 * pair : 2 * pair + 1], shifts[rows, 2 * pair + 1 : 2 * pair + 2]
-            )
+        own_shifts = own_offsets[rows, :].astype(jnp.int32)
+        partner_shifts = partner_offsets[rows, :].astype(jnp.int32)
+        work = ((tile(own), tile(prev), own_shifts[:, 2:4]), (tile(partner), chosen, partner_shifts[:, 0:2]))
+        for pair, (a_tile, b_tile, shifts) in enumerate(work):
+            found = offsets_found(a_tile, b_tile, shifts[:, 0:1], shifts[:, 1:2])
             for part in range(2):
                 at = 32 * (2 * pair + part) + ROWS * g + sublanes_of(ROWS)
                 row = row + jnp.where(lanes_of(ROWS) == at, found[part], 0.0)
@@ -114,8 +133,11 @@
     pay[0:1, :] = jnp.sum(row, axis=0, keepdims=True)
 
 
-def spread_kernel(own, below, above, out):
+def spread_kernel(place, own, odd_pairs, even_pairs, out):
     lane = lanes_of(1)
+    even = place[0] % 2 == 0
+    below = jnp.where(even, odd_pairs[...], even_pairs[...])
+    above = jnp.where(even, even_pairs[...], odd_pairs[...])
     conf = jnp.where(
         lane < 32,
         own[2:3, :],
@@ -264,34 +286,38 @@
     planes = lax.axis_size("z")
     count = planes * PLANE
     own = pixels[0]
+    swap = [(0, 1), (1, 0)]
     prev = lax.ppermute(own, SEC, [(i, i + 2) for i in range(count - 2)])
-    swap = [(0, 1), (1, 0)]
     partner = lax.ppermute(own, "core", swap)
-    partner_offsets = lax.ppermute(offsets[0, :, 0], "core", swap)
-    shifts = jnp.concatenate([offsets[1, :, 0], partner_offsets], 0).T
-    extra = jnp.zeros((8, LANES), jnp.float32)
-    extra = extra.at[1].set(connections.reshape(LANES).astype(jnp.float32))
-    extra = extra.at[2, :32].set(confidence[0])
     f32 = jnp.float32
+    place = jnp.stack([z, 2 * y + core, (LANES - 32 * x) % LANES, core]).astype(jnp.int32)
+    held, shifts, extra = pl.pallas_call(
+        prep_kernel,
+        out_shape=(pltpu.VMEM((32, PIX * PIX), jnp.bfloat16), pltpu.VMEM((32, LANES), f32), pltpu.VMEM((8, LANES), f32)),
+        in_specs=[VMEM] * 4,
+        out_specs=(VMEM, VMEM, VMEM),
+        name="prep",
+    )(own, offsets, connections, confidence)
+    partner_shifts = lax.ppermute(shifts, "core", swap)
 
     pay = pl.pallas_call(
         match_kernel,
         out_shape=pltpu.VMEM((8, LANES), f32),
-        in_specs=[SMEM] + [VMEM] * 5,
+        in_specs=[SMEM] + [VMEM] * 6,
         out_specs=VMEM,
         name="match",
-    )(core[None].astype(jnp.int32), *[kept(v) for v in (own, partner, prev, shifts, extra)])
-    below = lax.ppermute(pay, "z", [(i, i + 1) for i in range(planes - 1)])
-    above = lax.ppermute(pay, "z", [(i + 1, i) for i in range(planes - 1)])
+    )(place, *[kept(v) for v in (held, partner, prev, shifts, partner_shifts, extra)])
+    swaps = lambda first: [(i + d, i + 1 - d) for i in range(first, planes - 1, 2) for d in (0, 1)]
+    odd_pairs = lax.ppermute(pay, "z", swaps(1))
+    even_pairs = lax.ppermute(pay, "z", swaps(0))
     spread = pl.pallas_call(
         spread_kernel,
         out_shape=pltpu.VMEM((32, 8, LANES), f32),
-        in_specs=[VMEM] * 3,
+        in_specs=[SMEM] + [VMEM] * 3,
         out_specs=VMEM,
         name="spread",
-    )(kept(pay), kept(below), kept(above))
+    )(place, kept(pay), kept(odd_pairs), kept(even_pairs))
     gathered = lax.all_to_all(spread, ("y", "core", "x"), 0, 0, tiled=True)
-    place = jnp.stack([z, 2 * y + core, (LANES - 32 * x) % LANES]).astype(jnp.int32)
     sums, fields, measured = pl.pallas_call(
         relax_kernel,
         out_shape=(

time: 65.6 us -> 62 us (0.945)
  blocking collectives: 19.1 us -> 35.4 us
  waiting for transfers between devices: 12.2 us -> 2.24 us
  starting transfers between devices: 23.1 us -> 14.6 us
  local copies, waits for them, and re-layouts: 3.24 us -> 0 us
  Pallas kernels: 6.22 us -> 8.01 us
    all_to_all x0 -> x1, blocking collectives: none -> 13 us  [on_device(): gathered = lax.all_to_all(spread, ('y', 'core', 'x'), 0, 0, tiled=True)]
    all_to_all x1 -> x0, waiting for transfers between devices: 7.04 us -> none  [on_device(): gathered = lax.all_to_all(spread, ('y', 'core', 'x'), 0, 0, tiled=True)]
    all_to_all x1 -> x0, starting transfers between devices: 7.01 us -> none  [on_device(): gathered = lax.all_to_all(spread, ('y', 'core', 'x'), 0, 0, tiled=True)]
    all_to_all x1, blocking collectives: 19.1 us -> 22.4 us  [on_device(): lax.all_to_all(sums, 'z', 0, 0, tiled=True, axis_index_groups=turned)]
    ppermute x1, starting transfers between devices: 8.79 us -> 6.05 us  [on_device(): partner = lax.ppermute(own, 'core', swap)]
    ppermute x1, starting transfers between devices: 1.31 us -> 4.05 us  [on_device(): prev = lax.ppermute(own, SEC, [(i, i + 2) for i in range(count - 2)])]
    unnamed x6 -> x0, local copies, waits for them, and re-layouts: 2.27 us -> none
    ppermute x1, waiting for transfers between devices: 1.93 us -> 0.01 us  [on_device(): prev = lax.ppermute(own, SEC, [(i, i + 2) for i in range(count - 2)])]
  transfers between devices with their start and end apart: 6 -> 5, of which waited for: 3 -> 2; matrix products, arithmetic and copies ran while one was open for 2% -> 1% of each run, Pallas kernels for 0% -> 2%
where the time goes in v3:
time: 62 us; the launch traced here: 61.7 us
  blocking collectives  35.4 us (57%)
  starting transfers between devices  14.6 us (24%)
  Pallas kernels  8.01 us (13%)
  waiting for transfers between devices  2.24 us (4%)
  between operations  0.71 us (1%)
  other arithmetic  0.66 us (1%)
    all_to_all x1, blocking collectives, on_device(): lax.all_to_all(sums, 'z', 0, 0, tiled=True, axis_index_groups=turned)  22.4 us
    all_to_all x1, blocking collectives, on_device(): gathered = lax.all_to_all(spread, ('y', 'core', 'x'), 0, 0, tiled=True)  13 us
    ppermute x1, starting transfers between devices, on_device(): partner = lax.ppermute(own, 'core', swap)  6.05 us
    ppermute x1, starting transfers between devices, on_device(): prev = lax.ppermute(own, SEC, [(i, i + 2) for i in range(count - 2)])  4.05 us
    pallas_call x1, Pallas kernels, on_device(): pl.pallas_call(match_kernel, out_shape=pltpu.VMEM((8, LANES), f32), in_sp...  2.94 us
    pallas_call x1, Pallas kernels, on_device(): pl.pallas_call(relax_kernel, out_shape=(pltpu.VMEM((planes, 1, LANES), f3...  2.54 us
    ppermute x1, starting transfers between devices, on_device(): partner_shifts = lax.ppermute(shifts, 'core', swap)  1.92 us
    ppermute x1, starting transfers between devices, on_device(): even_pairs = lax.ppermute(pay, 'z', swaps(0))  1.92 us
  transfers between devices with their start and end apart: 5, of which 2 were waited for; matrix products, arithmetic and copies ran while one was open for 1% of the time, Pallas kernels for 2%

profile of v3, /device:TPU:1, one launch (start us, length us, event | category | flops | bytes accessed | tf_op | source)
XLA Modules:
  0.0 61.7 jit_solution(6420093240688169626)
XLA Ops:
  0.6 4.0 %collective-permute-start.1 = (bf16[32,4096]{1,0:T(8,128)(2,1)}, bf16[32,4096]{1,0:T(8,128)(2,1)S(1)}, u32[]{:S(2)}, u32[]{:S(2)}) collective-permute-start(bf16[32,4096]{1,0:T(8,128)(2,1)} %bitcast.7), channel_id=1, source_target_pairs={{0,8},{4,12},{8,16},{12,20},{16,24},{20,28},{24,32},{28,36},{32,40... | collective-permute-start | bytes 786440 | tf_op jit(solution)/shard_map/ppermute | solution.py:290
  4.7 6.0 %collective-permute-start = (bf16[32,4096]{1,0:T(8,128)(2,1)}, bf16[32,4096]{1,0:T(8,128)(2,1)S(1)}, u32[]{:S(2)}, u32[]{:S(2)}) collective-permute-start(bf16[32,4096]{1,0:T(8,128)(2,1)} %bitcast.8), channel_id=1, source_target_pairs={{0,4},{4,0},{1,5},{5,1},{2,6},{6,2},{3,7},{7,3},{8,12},{12,8},{9,1... | collective-permute-start | bytes 786440 | tf_op jit(solution)/shard_map/ppermute | solution.py:291
  10.7 1.1 %prep.1 = (bf16[32,4096]{1,0:T(8,128)(2,1)S(1)}, f32[32,128]{1,0:T(8,128)S(1)}, f32[8,128]{1,0:T(8,128)S(1)}) custom-call(bf16[32,4096]{1,0:T(8,128)(2,1)} %bitcast.9, s32[2,2,1,32]{3,2,1,0:T(1,128)} %offsets.1, s32[4,1,32]{2,1,0:T(1,128)} %connections.1, f32[1,32]{1,0:T(1,128)} %confidence.1), custom_call_target="tpu_custom_call" | custom-call | tf_op jit(solution)/shard_map/prep/pallas_call | solution.py:294
  11.8 1.9 %collective-permute-start.2 = (f32[32,128]{1,0:T(8,128)S(1)}, f32[32,128]{1,0:T(8,128)S(1)}, u32[]{:S(2)}, u32[]{:S(2)}) collective-permute-start(f32[32,128]{1,0:T(8,128)S(1)} %get-tuple-element.9.own_offsets), channel_id=1, source_target_pairs={{0,4},{4,0},{1,5},{5,1},{2,6},{6,2},{3,7},{7,3},{8,12},{12,8},{9,1... | collective-permute-start | bytes 49160 | tf_op jit(solution)/shard_map/ppermute | solution.py:301
  13.8 0.7 %pad_add_fusion.place = s32[4]{0:T(128)} fusion(s32[1]{0:T(128)} %bitcast.3, s32[1]{0:T(128)} %bitcast.2, s32[1]{0:T(128)} %bitcast.1, s32[1]{0:T(128)} %bitcast), kind=kLoop, calls=%fused_computation | loop fusion | flops 12 | bytes 32 | tf_op jit(solution)/shard_map/stack | solution.py:293
  14.4 0.5 collective-permute-done.2.partner_offsets
  14.9 0.0 collective-permute-done.1.prev
  14.9 0.0 collective-permute-done.partner
  14.9 2.9 %match.1.own = f32[8,128]{1,0:T(8,128)S(1)} custom-call(s32[4]{0:T(128)} %pad_add_fusion.place, bf16[32,4096]{1,0:T(8,128)(2,1)S(1)} %get-tuple-element.8.own, bf16[32,4096]{1,0:T(8,128)(2,1)S(1)} %collective-permute-done.partner, bf16[32,4096]{1,0:T(8,128)(2,1)S(1)} %collective-permute-done.1.prev, f32[32,128]{1,0:T(8,128)S(1)} %get-tuple-element.9.own_offsets, ...), custom_call_target="tpu_custom_call" | custom-call | tf_op jit(solution)/shard_map/match/pallas_call | solution.py:303
  17.9 1.9 %collective-permute-start.4 = (f32[8,128]{1,0:T(8,128)S(1)}, f32[8,128]{1,0:T(8,128)S(1)}, u32[]{:S(2)}, u32[]{:S(2)}) collective-permute-start(f32[8,128]{1,0:T(8,128)S(1)} %match.1.own), channel_id=1, source_target_pairs={{0,32},{32,0},{64,96},{96,64},{128,160},{160,128},{192,224},{224,1... | collective-permute-start | bytes 12296 | tf_op jit(solution)/shard_map/ppermute | solution.py:312
  19.8 0.7 %collective-permute-start.3 = (f32[8,128]{1,0:T(8,128)S(1)}, f32[8,128]{1,0:T(8,128)S(1)}, u32[]{:S(2)}, u32[]{:S(2)}) collective-permute-start(f32[8,128]{1,0:T(8,128)S(1)} %match.1.own), channel_id=1, source_target_pairs={{32,64},{64,32},{96,128},{128,96},{160,192},{192,160},{224,256},{2... | collective-permute-start | bytes 12296 | tf_op jit(solution)/shard_map/ppermute | solution.py:311
  20.5 1.8 %collective-permute-done.4.even_pairs = f32[8,128]{1,0:T(8,128)S(1)} collective-permute-done((f32[8,128]{1,0:T(8,128)S(1)}, f32[8,128]{1,0:T(8,128)S(1)}, u32[]{:S(2)}, u32[]{:S(2)}) %collective-permute-start.4) | collective-permute-done | bytes 4128 | tf_op jit(solution)/shard_map/ppermute | solution.py:312
  22.2 0.0 collective-permute-done.3.odd_pairs
  22.2 0.8 %spread.1 = f32[32,8,128]{2,1,0:T(8,128)S(1)} custom-call(s32[4]{0:T(128)} %pad_add_fusion.place, f32[8,128]{1,0:T(8,128)S(1)} %match.1.own, f32[8,128]{1,0:T(8,128)S(1)} %collective-permute-done.3.odd_pairs, f32[8,128]{1,0:T(8,128)S(1)} %collective-permute-done.4.even_pairs), custom_call_target="tpu_custom_call" | custom-call | tf_op jit(solution)/shard_map/spread/pallas_call | solution.py:313
  23.0 13.0 %all_to_all.10 = f32[32,8,128]{2,1,0:T(8,128)S(1)} all-to-all(f32[32,8,128]{2,1,0:T(8,128)S(1)} %spread.1), channel_id=1, replica_groups=mesh['z'=16,'y'=4,'core'=2,'x'=4] {'y','core','x'}, dimensions={0} | all-to-all | bytes 262144 | tf_op jit(solution)/shard_map/all_to_all | solution.py:320
  36.0 2.5 %relax.1 = (f32[16,1,128]{2,1,0:T(1,128)S(1)}, f32[8,128]{1,0:T(8,128)S(1)}, f32[2,2,1,32]{3,2,1,0:T(1,128)}) custom-call(s32[4]{0:T(128)} %pad_add_fusion.place, f32[256,128]{1,0:T(8,128)S(1)} %bitcast.6), custom_call_target="tpu_custom_call" | custom-call | tf_op jit(solution)/shard_map/relax/pallas_call | solution.py:321
  38.5 22.4 %all_to_all.11.sums = f32[16,1,128]{2,1,0:T(1,128)S(1)} all-to-all(f32[16,1,128]{2,1,0:T(1,128)S(1)} %get-tuple-element.12), channel_id=1, replica_groups={{256,288,320,352,384,416,448,480,0,32,64,96,128,160,192,224},{257,289,3..., dimensions={0} | all-to-all | bytes 16384 | tf_op jit(solution)/shard_map/all_to_all | solution.py:338
  61.0 0.7 %finish.1 = f32[2,1,32]{2,1,0:T(1,128)} custom-call(f32[16,1,128]{2,1,0:T(1,128)S(1)} %all_to_all.11.sums, f32[8,128]{1,0:T(8,128)S(1)} %get-tuple-element.13.fields), custom_call_target="tpu_custom_call" | custom-call | tf_op jit(solution)/shard_map/finish/pallas_call | solution.py:339
Async XLA Ops:
  0.6 14.3 %collective-permute-start.1 = (bf16[32,4096]{1,0:T(8,128)(2,1)}, bf16[32,4096]{1,0:T(8,128)(2,1)S(1)}, u32[]{:S(2)}, u32[]{:S(2)}) collective-permute-start(bf16[32,4096]{1,0:T(8,128)(2,1)} %bitcast.7), channel_id=1, source_target_pairs={{0,8},{4,12},{8,16},{12,20},{16,24},{20,28},{24,32},{28,36},{32,40... | collective-permute-start | bytes 786440 | tf_op jit(solution)/shard_map/ppermute | solution.py:290
  4.7 10.2 %collective-permute-start = (bf16[32,4096]{1,0:T(8,128)(2,1)}, bf16[32,4096]{1,0:T(8,128)(2,1)S(1)}, u32[]{:S(2)}, u32[]{:S(2)}) collective-permute-start(bf16[32,4096]{1,0:T(8,128)(2,1)} %bitcast.8), channel_id=1, source_target_pairs={{0,4},{4,0},{1,5},{5,1},{2,6},{6,2},{3,7},{7,3},{8,12},{12,8},{9,1... | collective-permute-start | bytes 786440 | tf_op jit(solution)/shard_map/ppermute | solution.py:291
  11.8 3.1 %collective-permute-start.2 = (f32[32,128]{1,0:T(8,128)S(1)}, f32[32,128]{1,0:T(8,128)S(1)}, u32[]{:S(2)}, u32[]{:S(2)}) collective-permute-start(f32[32,128]{1,0:T(8,128)S(1)} %get-tuple-element.9.own_offsets), channel_id=1, source_target_pairs={{0,4},{4,0},{1,5},{5,1},{2,6},{6,2},{3,7},{7,3},{8,12},{12,8},{9,1... | collective-permute-start | bytes 49160 | tf_op jit(solution)/shard_map/ppermute | solution.py:301
  17.9 4.4 %collective-permute-start.4 = (f32[8,128]{1,0:T(8,128)S(1)}, f32[8,128]{1,0:T(8,128)S(1)}, u32[]{:S(2)}, u32[]{:S(2)}) collective-permute-start(f32[8,128]{1,0:T(8,128)S(1)} %match.1.own), channel_id=1, source_target_pairs={{0,32},{32,0},{64,96},{96,64},{128,160},{160,128},{192,224},{224,1... | collective-permute-start | bytes 12296 | tf_op jit(solution)/shard_map/ppermute | solution.py:312
  19.8 2.4 %collective-permute-start.3 = (f32[8,128]{1,0:T(8,128)S(1)}, f32[8,128]{1,0:T(8,128)S(1)}, u32[]{:S(2)}, u32[]{:S(2)}) collective-permute-start(f32[8,128]{1,0:T(8,128)S(1)} %match.1.own), channel_id=1, source_target_pairs={{32,64},{64,32},{96,128},{128,96},{160,192},{192,160},{224,256},{2... | collective-permute-start | bytes 12296 | tf_op jit(solution)/shard_map/ppermute | solution.py:311

commit v4 on v3

--- a/solution.py
+++ b/solution.py
@@ -11,6 +11,8 @@
 TILES = PIX * PIX // LANES
 REACH = 4
 ROWS = 16
+HEAD = 24
+SUMS = 11
 PLANE = 8
 WINDOW = 3 * PLANE
 ANCHOR = 0.05
@@ -42,8 +44,8 @@
 
 
 def shifted_tiles(tile_of, shift_rows, lane):
-    steps = jnp.broadcast_to((shift_rows >> 1) + REACH, (ROWS, LANES))
-    odd_high = jnp.logical_and(jnp.broadcast_to(shift_rows & 1, (ROWS, LANES)) == 1, lane >= PIX)
+    steps = (shift_rows >> 1) + REACH
+    odd_high = jnp.logical_and((shift_rows & 1) == 1, lane >= PIX)
     tiles = [tile_of((j + REACH) % TILES) for j in range(TILES)]
     for bit in range(4):
         move = (steps & (1 << bit)) != 0
@@ -51,86 +53,112 @@
     return [jnp.where(odd_high, tiles[j - 1], tiles[j]) for j in range(TILES)]
 
 
-def offsets_found(a_tile, b_tile, shift_rows, shift_cols):
+def products(a_tile, b_tile, shift_rows, shift_cols):
     lane = lanes_of(ROWS)
     low = lane < PIX
     moved = shifted_tiles(b_tile, shift_rows, lane)
     half = (lane ^ (PIX * (shift_rows & 1))) & PIX
     index = [half | ((lane - shift_cols - e) & (PIX - 1)) for e in (-1, 0, 1)]
     rolled = lambda j: pltpu.roll(a_tile(j % TILES), PIX, 1)
-    zero = jnp.zeros((ROWS, LANES), jnp.float32)
-    sums = [[zero] * 3 for _ in range(3)]
-    energy_a, energy_b = zero, zero
+    sums = [jnp.zeros((ROWS, LANES), jnp.float32)] * SUMS
     before, here = rolled(TILES - 1), rolled(0)
     for j in range(TILES):
         after = rolled(j + 1)
         centre = a_tile(j)
         rows_a = (jnp.where(low, before, here), centre, jnp.where(low, here, after))
         cols_b = [pick_rows(moved[j], index[e]) for e in range(3)]
-        for e1 in range(3):
-            for e2 in range(3):
-                sums[e1][e2] = sums[e1][e2] + rows_a[e1] * cols_b[e2]
-        energy_a = energy_a + centre * centre
-        energy_b = energy_b + cols_b[1] * cols_b[1]
+        terms = [rows_a[e1] * cols_b[e2] for e1 in range(3) for e2 in range(3)]
+        terms += [centre * centre, cols_b[1] * cols_b[1]]
+        sums = [total + term for total, term in zip(sums, terms)]
         before, here = here, after
-    total = lambda v: jnp.sum(v, axis=1, keepdims=True)
-    scale = (total(energy_a) / PIX**2 + 1e-05) * (total(energy_b) / PIX**2 + 1e-05) * PIX**2
-    weights = []
-    for e1 in range(3):
-        corr = [total(sums[e1][e2]) for e2 in range(3)]
-        weights.append([c * c / scale for c in corr])
-    row_sums = [weights[e][0] + weights[e][1] + weights[e][2] for e in range(3)]
-    summed = 1.0 + row_sums[0] + row_sums[1] + row_sums[2]
-    col_low = weights[0][0] + weights[1][0] + weights[2][0]
-    col_high = weights[0][2] + weights[1][2] + weights[2][2]
-    return (
-        shift_rows.astype(jnp.float32) + (row_sums[2] - row_sums[0]) / summed,
-        shift_cols.astype(jnp.float32) + (col_high - col_low) / summed,
+    return sums
+
+
+def tile_reader(refs, group):
+    rows = slice(ROWS * group, ROWS * (group + 1))
+
+    def tile(j):
+        ref, j = (refs[0], j) if len(refs) == 1 or j < HEAD else (refs[1], j - HEAD)
+        return ref[rows, LANES * j : LANES * (j + 1)].astype(jnp.float32)
+
+    return tile
+
+
+def pair_products(out, at, a_refs, b_refs, turn):
+    for g in range(2):
+        rows = slice(ROWS * g, ROWS * (g + 1))
+        sums = products(tile_reader(a_refs, g), tile_reader(b_refs, g), turn(0, rows), turn(1, rows))
+        for k in range(SUMS):
+            out[k, at + ROWS * g : at + ROWS * (g + 1), :] = sums[k]
+
+
+def own_turns(turn):
+    return lambda part, rows: turn[32 * part + rows.start : 32 * part + rows.stop, :]
+
+
+def sent_turns(tail):
+    at = PIX * PIX - LANES * HEAD
+    return lambda part, rows: (
+        tail[rows, at + LANES * part : at + LANES * (part + 1)].astype(jnp.float32).astype(jnp.int32)
     )
 
 
-def prep_kernel(pixels, offsets, connections, confidence, own, shifts, extra):
+def prep_kernel(pixels, offsets, connections, confidence, own, head, tail, turn, extra):
+    cut = LANES * HEAD
+    rest = PIX * PIX - cut
     own[...] = pixels[...]
-    rows = sublanes_of(ROWS)
-    lane = lanes_of(ROWS)
-    for g in range(2):
-        tile = jnp.zeros((ROWS, LANES), jnp.float32)
-        for d in range(2):
-            for part in range(2):
-                row = offsets[d, part].astype(jnp.float32)
-                chosen = jnp.where(lane[:, :32] == rows[:, :32] + ROWS * g, row, 0.0)
-                tile = jnp.where(lane == 2 * d + part, jnp.sum(chosen, axis=1, keepdims=True), tile)
-        shifts[ROWS * g : ROWS * (g + 1), :] = tile
+    head[...] = pixels[:, 0:cut]
+    tail[:, 0:rest] = pixels[:, cut:]
+    patch = lax.broadcasted_iota(jnp.int32, (32, 32), 0)
+    diagonal = patch == lax.broadcasted_iota(jnp.int32, (32, 32), 1)
+    for d in range(2):
+        for part in range(2):
+            chosen = jnp.where(diagonal, offsets[d, part].astype(jnp.float32), 0.0)
+            column = jnp.broadcast_to(jnp.sum(chosen, axis=1, keepdims=True), (32, LANES))
+            if d == 0:
+                tail[:, rest + LANES * part : rest + LANES * (part + 1)] = column.astype(jnp.bfloat16)
+            else:
+                turn[32 * part : 32 * (part + 1), :] = column.astype(jnp.int32)
     extra[...] = jnp.zeros_like(extra)
     for j in range(4):
         extra[1:2, 32 * j : 32 * (j + 1)] = connections[j].astype(jnp.float32)
     extra[2:3, 0:32] = confidence[...]
 
 
-def match_kernel(place, own, partner, prev, own_offsets, partner_offsets, extra, pay):
-    first_core = place[3] == 0
-
-    def group(g, row):
-        rows = pl.ds(pl.multiple_of(ROWS * g, ROWS), ROWS)
-        tile = lambda ref: lambda j: ref[rows, LANES * j : LANES * (j + 1)].astype(jnp.float32)
-
-        def chosen(j):
-            at = (rows, slice(LANES * j, LANES * (j + 1)))
-            return jnp.where(first_core, own[at].astype(jnp.float32), prev[at].astype(jnp.float32))
-
-        own_shifts = own_offsets[rows, :].astype(jnp.int32)
-        partner_shifts = partner_offsets[rows, :].astype(jnp.int32)
-        work = ((tile(own), tile(prev), own_shifts[:, 2:4]), (tile(partner), chosen, partner_shifts[:, 0:2]))
-        for pair, (a_tile, b_tile, shifts) in enumerate(work):
-            found = offsets_found(a_tile, b_tile, shifts[:, 0:1], shifts[:, 1:2])
-            for part in range(2):
-                at = 32 * (2 * pair + part) + ROWS * g + sublanes_of(ROWS)
-                row = row + jnp.where(lanes_of(ROWS) == at, found[part], 0.0)
-        return row
-
-    row = lax.fori_loop(0, 2, group, jnp.zeros((ROWS, LANES), jnp.float32))
+def chip_kernel(place, own, head, tail, ready):
+    @pl.when(place[3] == 0)
+    def _():
+        pair_products(ready, 0, (head, tail), (own,), sent_turns(tail))
+
+
+def match_kernel(place, head, tail, prev, own, turn, ready, extra, pay, sums):
+    @pl.when(place[3] == 0)
+    def _():
+        sums[:, 32:64, :] = ready[...]
+
+    @pl.when(place[3] != 0)
+    def _():
+        pair_products(sums, 32, (head, tail), (prev,), sent_turns(tail))
+
+    pair_products(sums, 0, (own,), (prev,), own_turns(turn))
+    total = [jnp.sum(sums[k], axis=1, keepdims=True) for k in range(SUMS)]
+    scale = (total[9] / PIX**2 + 1e-05) * (total[10] / PIX**2 + 1e-05) * PIX**2
+    inverse = 1.0 / scale
+    weights = [[total[3 * e1 + e2] * total[3 * e1 + e2] * inverse for e2 in range(3)] for e1 in range(3)]
+    row_sums = [weights[e][0] + weights[e][1] + weights[e][2] for e in range(3)]
+    share = 1.0 / (1.0 + row_sums[0] + row_sums[1] + row_sums[2])
+    col_low = weights[0][0] + weights[1][0] + weights[2][0]
+    col_high = weights[0][2] + weights[1][2] + weights[2][2]
+    shifts = [
+        jnp.concatenate([turns(part, slice(0, 32)) for turns in (own_turns(turn), sent_turns(tail))], 0).astype(jnp.float32)
+        for part in range(2)
+    ]
+    found_rows = shifts[0] + (row_sums[2] - row_sums[0]) * share
+    found_cols = shifts[1] + (col_high - col_low) * share
+    lane, pair = lanes_of(64), sublanes_of(64)
+    line = jnp.where(lane == pair, found_rows, jnp.where(lane == 64 + pair, found_cols, 0.0))
     pay[...] = extra[...]
-    pay[0:1, :] = jnp.sum(row, axis=0, keepdims=True)
+    pay[0:1, :] = jnp.sum(line, axis=0, keepdims=True)
 
 
 def spread_kernel(place, own, odd_pairs, even_pairs, out):
@@ -149,7 +177,7 @@
     out[...] = jnp.broadcast_to(jnp.concatenate(rows, 0)[None], out.shape)
 
 
-def relax_kernel(place, gathered, sums_out, fields_out, measured_out, links, left, pushed):
+def relax_kernel(place, gathered, sums_out, fields_out, links, left, pushed):
     lane = lanes_of(PLANE)
     sub = sublanes_of(PLANE)
 
@@ -172,7 +200,7 @@
     down = lambda v, k: pltpu.roll(v, k, 0)
 
     found = [window([(2, q), (0, q), (4, q)]) for q in range(4)]
-    measured = {1: [cores_swapped(found[2]), cores_swapped(found[3])], 2: found[:2]}
+    measured = {1: [cores_swapped(found[1]), cores_swapped(found[3])], 2: [found[0], found[2]]}
     node_links = [window([(3, q), (1, q), (5, q)]).astype(jnp.int32) for q in range(4)]
     confidence = window([(6, 1), (6, 0), (6, 2)])
     section = PLANE * (place[0] - 1) + sublanes_of(WINDOW)
@@ -255,13 +283,15 @@
         return pltpu.roll(row, place[2], 1)
 
     fields = [own(f[c]) for f in (start, once, twice) for c in range(2)]
-    fields_out[...] = jnp.concatenate(fields + [jnp.zeros((2, LANES), jnp.float32)], 0)
-    for d in (1, 2):
+    fields += [own(measured[d][c]) for d in (1, 2) for c in range(2)]
+    fields_out[...] = jnp.concatenate(fields + [jnp.zeros((6, LANES), jnp.float32)], 0)
+
+
+def finish_kernel(sums, fields, measured_out, out):
+    for d in range(2):
         for c in range(2):
-            measured_out[d - 1, c] = own(measured[d][c])[:, :32]
-
-
-def finish_kernel(sums, fields, out):
+            row = 6 + 2 * d + c
+            measured_out[d, c] = fields[row : row + 1, 0:32]
     line = jnp.sum(sums[...], axis=0)
     lane = lanes_of(1)
     m = [jnp.sum(jnp.where(lane == k, line, 0.0), axis=1, keepdims=True) for k in range(6)]
@@ -288,25 +318,37 @@
     own = pixels[0]
     swap = [(0, 1), (1, 0)]
     prev = lax.ppermute(own, SEC, [(i, i + 2) for i in range(count - 2)])
-    partner = lax.ppermute(own, "core", swap)
     f32 = jnp.float32
     place = jnp.stack([z, 2 * y + core, (LANES - 32 * x) % LANES, core]).astype(jnp.int32)
-    held, shifts, extra = pl.pallas_call(
+    held, head, tail, turn, extra = pl.pallas_call(
         prep_kernel,
-        out_shape=(pltpu.VMEM((32, PIX * PIX), jnp.bfloat16), pltpu.VMEM((32, LANES), f32), pltpu.VMEM((8, LANES), f32)),
+        out_shape=(
+            pltpu.VMEM((32, PIX * PIX), jnp.bfloat16),
+            pltpu.VMEM((32, LANES * HEAD), jnp.bfloat16),
+            pltpu.VMEM((32, PIX * PIX - LANES * HEAD + 2 * LANES), jnp.bfloat16),
+            pltpu.VMEM((64, LANES), jnp.int32),
+            pltpu.VMEM((8, LANES), f32),
+        ),
         in_specs=[VMEM] * 4,
-        out_specs=(VMEM, VMEM, VMEM),
+        out_specs=(VMEM,) * 5,
         name="prep",
     )(own, offsets, connections, confidence)
-    partner_shifts = lax.ppermute(shifts, "core", swap)
-
+    head, tail = (lax.ppermute(v, "core", swap) for v in (head, tail))
+    ready = pl.pallas_call(
+        chip_kernel,
+        out_shape=pltpu.VMEM((SUMS, 32, LANES), f32),
+        in_specs=[SMEM] + [VMEM] * 3,
+        out_specs=VMEM,
+        name="chip",
+    )(place, kept(held), kept(head), kept(tail))
     pay = pl.pallas_call(
         match_kernel,
         out_shape=pltpu.VMEM((8, LANES), f32),
-        in_specs=[SMEM] + [VMEM] * 6,
+        in_specs=[SMEM] + [VMEM] * 7,
         out_specs=VMEM,
+        scratch_shapes=[pltpu.VMEM((SUMS, 64, LANES), f32)],
         name="match",
-    )(place, *[kept(v) for v in (held, partner, prev, shifts, partner_shifts, extra)])
+    )(place, *[kept(v) for v in (head, tail, prev, held, turn, ready, extra)])
     swaps = lambda first: [(i + d, i + 1 - d) for i in range(first, planes - 1, 2) for d in (0, 1)]
     odd_pairs = lax.ppermute(pay, "z", swaps(1))
     even_pairs = lax.ppermute(pay, "z", swaps(0))
@@ -318,15 +360,14 @@
         name="spread",
     )(place, kept(pay), kept(odd_pairs), kept(even_pairs))
     gathered = lax.all_to_all(spread, ("y", "core", "x"), 0, 0, tiled=True)
-    sums, fields, measured = pl.pallas_call(
+    sums, fields = pl.pallas_call(
         relax_kernel,
         out_shape=(
             pltpu.VMEM((planes, 1, LANES), f32),
-            pltpu.VMEM((8, LANES), f32),
-            jax.ShapeDtypeStruct((2, 2, 1, 32), f32),
+            pltpu.VMEM((16, LANES), f32),
         ),
         in_specs=[SMEM, VMEM],
-        out_specs=(VMEM, VMEM, VMEM),
+        out_specs=(VMEM, VMEM),
         scratch_shapes=[
             pltpu.VMEM((14, LANES, LANES), jnp.bfloat16),
             pltpu.VMEM((WINDOW * 8, LANES), f32),
@@ -336,11 +377,11 @@
     )(place, kept(gathered.reshape(32 * 8, LANES)))
     turned = [[(i + planes // 2) % planes for i in range(planes)]]
     everywhere = lax.all_to_all(sums, "z", 0, 0, tiled=True, axis_index_groups=turned)
-    displacement = pl.pallas_call(
+    measured, displacement = pl.pallas_call(
         finish_kernel,
-        out_shape=jax.ShapeDtypeStruct((2, 1, 32), f32),
+        out_shape=(jax.ShapeDtypeStruct((2, 2, 1, 32), f32), jax.ShapeDtypeStruct((2, 1, 32), f32)),
         in_specs=[VMEM] * 2,
-        out_specs=VMEM,
+        out_specs=(VMEM, VMEM),
         name="finish",
     )(kept(everywhere), kept(fields))
     return (measured, displacement)

time: 62 us -> 61 us (0.984)
  starting transfers between devices: 14.6 us -> 16.2 us
  blocking collectives: 35.4 us -> 33.9 us
  waiting for transfers between devices: 2.24 us -> 1.55 us
    all_to_all x1, blocking collectives: 22.4 us -> 18.6 us  [on_device(): lax.all_to_all(sums, 'z', 0, 0, tiled=True, axis_index_groups=turned)]
    all_to_all x1, blocking collectives: 13 us -> 15.3 us  [on_device(): gathered = lax.all_to_all(spread, ('y', 'core', 'x'), 0, 0, tiled=True)]
    ppermute x1, starting transfers between devices: 1.92 us -> 3.56 us  [on_device(): even_pairs = lax.ppermute(pay, 'z', swaps(0))]
    ppermute x1, waiting for transfers between devices: 1.75 us -> 0.97 us  [on_device(): even_pairs = lax.ppermute(pay, 'z', swaps(0))]
    pallas_call x1 -> x2, Pallas kernels: 0.7 us -> 1.37 us  [the longest x1 0.7 us: on_device(): pl.pallas_call(finish_kernel, out_shape=(jax.ShapeDtypeStruct((2, 2, 1, 3...]
  transfers between devices with their start and end apart: 5 -> 5, of which waited for: 2 -> 2; matrix products, arithmetic and copies ran while one was open for 1% -> 1% of each run, Pallas kernels for 2% -> 3%
where the time goes in v4:
time: 61 us; the launch traced here: 60.6 us
  blocking collectives  33.9 us (56%)
  starting transfers between devices  16.2 us (27%)
  Pallas kernels  7.56 us (12%)
  waiting for transfers between devices  1.55 us (3%)
  between operations  0.74 us (1%)
  other arithmetic  0.66 us (1%)
    all_to_all x1, blocking collectives, on_device(): lax.all_to_all(sums, 'z', 0, 0, tiled=True, axis_index_groups=turned)  18.6 us
    all_to_all x1, blocking collectives, on_device(): gathered = lax.all_to_all(spread, ('y', 'core', 'x'), 0, 0, tiled=True)  15.3 us
    ppermute x2, starting transfers between devices, on_device(): head, tail = (lax.ppermute(v, 'core', swap) for v in (head, tail))  7.97 us
    ppermute x1, starting transfers between devices, on_device(): prev = lax.ppermute(own, SEC, [(i, i + 2) for i in range(count - 2)])  4.05 us
    ppermute x1, starting transfers between devices, on_device(): even_pairs = lax.ppermute(pay, 'z', swaps(0))  3.56 us
    pallas_call x1, Pallas kernels, on_device(): pl.pallas_call(match_kernel, out_shape=pltpu.VMEM((8, LANES), f32), in_sp...  2.39 us
    pallas_call x1, Pallas kernels, on_device(): pl.pallas_call(relax_kernel, out_shape=(pltpu.VMEM((planes, 1, LANES), f3...  1.95 us
  transfers between devices with their start and end apart: 5, of which 2 were waited for; matrix products, arithmetic and copies ran while one was open for 1% of the time, Pallas kernels for 3%

profile of v4, /device:TPU:1, one launch (start us, length us, event | category | flops | bytes accessed | tf_op | source)
XLA Modules:
  0.0 60.6 jit_solution(15504954349369807156)
XLA Ops:
  0.6 4.0 %collective-permute-start.2 = (bf16[32,4096]{1,0:T(8,128)(2,1)}, bf16[32,4096]{1,0:T(8,128)(2,1)S(1)}, u32[]{:S(2)}, u32[]{:S(2)}) collective-permute-start(bf16[32,4096]{1,0:T(8,128)(2,1)} %bitcast.7), channel_id=1, source_target_pairs={{0,8},{4,12},{8,16},{12,20},{16,24},{20,28},{24,32},{28,36},{32,40... | collective-permute-start | bytes 786440 | tf_op jit(solution)/shard_map/ppermute | solution.py:320
  4.7 1.1 %prep.1 = (bf16[32,4096]{1,0:T(8,128)(2,1)S(1)}, bf16[32,3072]{1,0:T(8,128)(2,1)S(1)}, bf16[32,1280]{1,0:T(8,128)(2,1)S(1)}, s32[64,128]{1,0:T(8,128)S(1)}, f32[8,128]{1,0:T(8,128)S(1)}) custom-call(bf16[32,4096]{1,0:T(8,128)(2,1)} %bitcast.8, s32[2,2,1,32]{3,2,1,0:T(1,128)} %offsets.1, s32[4,1,32]{2,1,0:T(1,128)} %connections.1, f32[1,32]{1,0:T(1,128)} %confidence.1), custom_call_target="tpu_custom_call" | custom-call | tf_op jit(solution)/shard_map/prep/pallas_call | solution.py:323
  5.8 6.0 %collective-permute-start = (bf16[32,3072]{1,0:T(8,128)(2,1)S(1)}, bf16[32,3072]{1,0:T(8,128)(2,1)S(1)}, u32[]{:S(2)}, u32[]{:S(2)}) collective-permute-start(bf16[32,3072]{1,0:T(8,128)(2,1)S(1)} %get-tuple-element.9), channel_id=1, source_target_pairs={{0,4},{4,0},{1,5},{5,1},{2,6},{6,2},{3,7},{7,3},{8,12},{12,8},{9,1... | collective-permute-start | bytes 589832 | tf_op jit(solution)/shard_map/ppermute | solution.py:336
  11.8 1.9 %collective-permute-start.1 = (bf16[32,1280]{1,0:T(8,128)(2,1)S(1)}, bf16[32,1280]{1,0:T(8,128)(2,1)S(1)}, u32[]{:S(2)}, u32[]{:S(2)}) collective-permute-start(bf16[32,1280]{1,0:T(8,128)(2,1)S(1)} %get-tuple-element.10), channel_id=1, source_target_pairs={{0,4},{4,0},{1,5},{5,1},{2,6},{6,2},{3,7},{7,3},{8,12},{12,8},{9,1... | collective-permute-start | bytes 245768 | tf_op jit(solution)/shard_map/ppermute | solution.py:336
  13.8 0.7 %pad_add_fusion.place = s32[4]{0:T(128)} fusion(s32[1]{0:T(128)} %bitcast.3, s32[1]{0:T(128)} %bitcast.2, s32[1]{0:T(128)} %bitcast.1, s32[1]{0:T(128)} %bitcast), kind=kLoop, calls=%fused_computation | loop fusion | flops 12 | bytes 32 | tf_op jit(solution)/shard_map/stack | solution.py:322
  14.4 0.6 collective-permute-done.1.tail
  15.0 0.0 collective-permute-done.head
  15.0 0.7 %chip.1.ready = f32[11,32,128]{2,1,0:T(8,128)S(1)} custom-call(s32[4]{0:T(128)} %pad_add_fusion.place, bf16[32,4096]{1,0:T(8,128)(2,1)S(1)} %get-tuple-element.11.own, bf16[32,3072]{1,0:T(8,128)(2,1)S(1)} %collective-permute-done.head, bf16[32,1280]{1,0:T(8,128)(2,1)S(1)} %collective-permute-done.1.tail), custom_call_target="tpu_custom_call" | custom-call | tf_op jit(solution)/shard_map/chip/pallas_call | solution.py:337
  15.7 0.0 collective-permute-done.2.prev
  15.7 2.4 %match.1.own = f32[8,128]{1,0:T(8,128)S(1)} custom-call(s32[4]{0:T(128)} %pad_add_fusion.place, bf16[32,3072]{1,0:T(8,128)(2,1)S(1)} %collective-permute-done.head, bf16[32,1280]{1,0:T(8,128)(2,1)S(1)} %collective-permute-done.1.tail, bf16[32,4096]{1,0:T(8,128)(2,1)S(1)} %collective-permute-done.2.prev, bf16[32,4096]{1,0:T(8,128)(2,1)S(1)} %get-tuple-element.11.own, ...), custom_call_target="tpu_custom_call" | custom-call | tf_op jit(solution)/shard_map/match/pallas_call | solution.py:344
  18.1 0.7 %collective-permute-start.3 = (f32[8,128]{1,0:T(8,128)S(1)}, f32[8,128]{1,0:T(8,128)S(1)}, u32[]{:S(2)}, u32[]{:S(2)}) collective-permute-start(f32[8,128]{1,0:T(8,128)S(1)} %match.1.own), channel_id=1, source_target_pairs={{32,64},{64,32},{96,128},{128,96},{160,192},{192,160},{224,256},{2... | collective-permute-start | bytes 12296 | tf_op jit(solution)/shard_map/ppermute | solution.py:353
  18.8 3.6 %collective-permute-start.4 = (f32[8,128]{1,0:T(8,128)S(1)}, f32[8,128]{1,0:T(8,128)S(1)}, u32[]{:S(2)}, u32[]{:S(2)}) collective-permute-start(f32[8,128]{1,0:T(8,128)S(1)} %match.1.own), channel_id=1, source_target_pairs={{0,32},{32,0},{64,96},{96,64},{128,160},{160,128},{192,224},{224,1... | collective-permute-start | bytes 12296 | tf_op jit(solution)/shard_map/ppermute | solution.py:354
  22.3 0.0 collective-permute-done.3.odd_pairs
  22.4 1.0 %collective-permute-done.4.even_pairs = f32[8,128]{1,0:T(8,128)S(1)} collective-permute-done((f32[8,128]{1,0:T(8,128)S(1)}, f32[8,128]{1,0:T(8,128)S(1)}, u32[]{:S(2)}, u32[]{:S(2)}) %collective-permute-start.4) | collective-permute-done | bytes 4128 | tf_op jit(solution)/shard_map/ppermute | solution.py:354
  23.3 0.8 %spread.1 = f32[32,8,128]{2,1,0:T(8,128)S(1)} custom-call(s32[4]{0:T(128)} %pad_add_fusion.place, f32[8,128]{1,0:T(8,128)S(1)} %match.1.own, f32[8,128]{1,0:T(8,128)S(1)} %collective-permute-done.3.odd_pairs, f32[8,128]{1,0:T(8,128)S(1)} %collective-permute-done.4.even_pairs), custom_call_target="tpu_custom_call" | custom-call | tf_op jit(solution)/shard_map/spread/pallas_call | solution.py:355
  24.1 15.3 %all_to_all.10 = f32[32,8,128]{2,1,0:T(8,128)S(1)} all-to-all(f32[32,8,128]{2,1,0:T(8,128)S(1)} %spread.1), channel_id=1, replica_groups=mesh['z'=16,'y'=4,'core'=2,'x'=4] {'y','core','x'}, dimensions={0} | all-to-all | bytes 262144 | tf_op jit(solution)/shard_map/all_to_all | solution.py:362
  39.4 2.0 %relax.1 = (f32[16,1,128]{2,1,0:T(1,128)S(1)}, f32[16,128]{1,0:T(8,128)S(1)}) custom-call(s32[4]{0:T(128)} %pad_add_fusion.place, f32[256,128]{1,0:T(8,128)S(1)} %bitcast.6), custom_call_target="tpu_custom_call" | custom-call | tf_op jit(solution)/shard_map/relax/pallas_call | solution.py:363
  41.4 18.6 %all_to_all.11.sums = f32[16,1,128]{2,1,0:T(1,128)S(1)} all-to-all(f32[16,1,128]{2,1,0:T(1,128)S(1)} %get-tuple-element.14), channel_id=1, replica_groups={{256,288,320,352,384,416,448,480,0,32,64,96,128,160,192,224},{257,289,3..., dimensions={0} | all-to-all | bytes 16384 | tf_op jit(solution)/shard_map/all_to_all | solution.py:379
  59.9 0.7 %finish.1 = (f32[2,2,1,32]{3,2,1,0:T(1,128)}, f32[2,1,32]{2,1,0:T(1,128)}) custom-call(f32[16,1,128]{2,1,0:T(1,128)S(1)} %all_to_all.11.sums, f32[16,128]{1,0:T(8,128)S(1)} %get-tuple-element.15.fields), custom_call_target="tpu_custom_call" | custom-call | tf_op jit(solution)/shard_map/finish/pallas_call | solution.py:380
Async XLA Ops:
  0.6 15.1 %collective-permute-start.2 = (bf16[32,4096]{1,0:T(8,128)(2,1)}, bf16[32,4096]{1,0:T(8,128)(2,1)S(1)}, u32[]{:S(2)}, u32[]{:S(2)}) collective-permute-start(bf16[32,4096]{1,0:T(8,128)(2,1)} %bitcast.7), channel_id=1, source_target_pairs={{0,8},{4,12},{8,16},{12,20},{16,24},{20,28},{24,32},{28,36},{32,40... | collective-permute-start | bytes 786440 | tf_op jit(solution)/shard_map/ppermute | solution.py:320
  5.8 9.2 %collective-permute-start = (bf16[32,3072]{1,0:T(8,128)(2,1)S(1)}, bf16[32,3072]{1,0:T(8,128)(2,1)S(1)}, u32[]{:S(2)}, u32[]{:S(2)}) collective-permute-start(bf16[32,3072]{1,0:T(8,128)(2,1)S(1)} %get-tuple-element.9), channel_id=1, source_target_pairs={{0,4},{4,0},{1,5},{5,1},{2,6},{6,2},{3,7},{7,3},{8,12},{12,8},{9,1... | collective-permute-start | bytes 589832 | tf_op jit(solution)/shard_map/ppermute | solution.py:336
  11.8 3.2 %collective-permute-start.1 = (bf16[32,1280]{1,0:T(8,128)(2,1)S(1)}, bf16[32,1280]{1,0:T(8,128)(2,1)S(1)}, u32[]{:S(2)}, u32[]{:S(2)}) collective-permute-start(bf16[32,1280]{1,0:T(8,128)(2,1)S(1)} %get-tuple-element.10), channel_id=1, source_target_pairs={{0,4},{4,0},{1,5},{5,1},{2,6},{6,2},{3,7},{7,3},{8,12},{12,8},{9,1... | collective-permute-start | bytes 245768 | tf_op jit(solution)/shard_map/ppermute | solution.py:336
  18.1 4.2 %collective-permute-start.3 = (f32[8,128]{1,0:T(8,128)S(1)}, f32[8,128]{1,0:T(8,128)S(1)}, u32[]{:S(2)}, u32[]{:S(2)}) collective-permute-start(f32[8,128]{1,0:T(8,128)S(1)} %match.1.own), channel_id=1, source_target_pairs={{32,64},{64,32},{96,128},{128,96},{160,192},{192,160},{224,256},{2... | collective-permute-start | bytes 12296 | tf_op jit(solution)/shard_map/ppermute | solution.py:353
  18.8 4.6 %collective-permute-start.4 = (f32[8,128]{1,0:T(8,128)S(1)}, f32[8,128]{1,0:T(8,128)S(1)}, u32[]{:S(2)}, u32[]{:S(2)}) collective-permute-start(f32[8,128]{1,0:T(8,128)S(1)} %match.1.own), channel_id=1, source_target_pairs={{0,32},{32,0},{64,96},{96,64},{128,160},{160,128},{192,224},{224,1... | collective-permute-start | bytes 12296 | tf_op jit(solution)/shard_map/ppermute | solution.py:354

commit v5 on v4

--- a/solution.py
+++ b/solution.py
@@ -14,12 +14,12 @@
 HEAD = 24
 SUMS = 11
 PLANE = 8
+LEADER = 22
 WINDOW = 3 * PLANE
 ANCHOR = 0.05
 SPRINGS = ((1, 1.0), (2, 0.5))
 SEC = ("z", "y", "core")
 VMEM = pl.BlockSpec(memory_space=pltpu.VMEM)
-SMEM = pl.BlockSpec(memory_space=pltpu.SMEM)
 
 
 def kept(array):
@@ -122,21 +122,24 @@
     extra[...] = jnp.zeros_like(extra)
     for j in range(4):
         extra[1:2, 32 * j : 32 * (j + 1)] = connections[j].astype(jnp.float32)
-    extra[2:3, 0:32] = confidence[...]
-
-
-def chip_kernel(place, own, head, tail, ready):
-    @pl.when(place[3] == 0)
+    for k in range(3):
+        extra[2 + k : 3 + k, 32 * k : 32 * (k + 1)] = confidence[...]
+
+
+def chip_kernel(own, head, tail, ready):
+    @pl.when(lax.axis_index("core") == 0)
     def _():
         pair_products(ready, 0, (head, tail), (own,), sent_turns(tail))
 
 
-def match_kernel(place, head, tail, prev, own, turn, ready, extra, pay, sums):
-    @pl.when(place[3] == 0)
+def match_kernel(head, tail, prev, own, turn, ready, extra, pay, sums):
+    core = lax.axis_index("core")
+
+    @pl.when(core == 0)
     def _():
         sums[:, 32:64, :] = ready[...]
 
-    @pl.when(place[3] != 0)
+    @pl.when(core != 0)
     def _():
         pair_products(sums, 32, (head, tail), (prev,), sent_turns(tail))
 
@@ -161,36 +164,35 @@
     pay[0:1, :] = jnp.sum(line, axis=0, keepdims=True)
 
 
-def spread_kernel(place, own, odd_pairs, even_pairs, out):
-    lane = lanes_of(1)
-    even = place[0] % 2 == 0
-    below = jnp.where(even, odd_pairs[...], even_pairs[...])
-    above = jnp.where(even, even_pairs[...], odd_pairs[...])
-    conf = jnp.where(
-        lane < 32,
-        own[2:3, :],
-        jnp.where(
-            lane < 64, pltpu.roll(below[2:3, :], 32, 1), jnp.where(lane < 96, pltpu.roll(above[2:3, :], 64, 1), 0.0)
-        ),
-    )
-    rows = [own[0:2, :], below[0:2, :], above[0:2, :], conf, jnp.zeros((1, LANES), jnp.float32)]
-    out[...] = jnp.broadcast_to(jnp.concatenate(rows, 0)[None], out.shape)
-
-
-def relax_kernel(place, gathered, sums_out, fields_out, links, left, pushed):
+def relax_kernel(gathered, sums_out, fields_out, links, left, pushed):
     lane = lanes_of(PLANE)
     sub = sublanes_of(PLANE)
 
-    def assembled(row, quarter):
+    z, y, core, x_own = (lax.axis_index(name) for name in ("z", "y", "core", "x"))
+    even = z % 2 == 0
+
+    def loaded(row):
+        found = [gathered[pl.ds(8 * x + row, PLANE, stride=32), :] for x in range(4)]
+        section, x = LEADER // 4, LEADER % 4
+        first, other = found[0], found[x]
+        found[0] = jnp.where(sub == 0, pltpu.roll(other, PLANE - section, 0), first)
+        found[x] = jnp.where(sub == section, pltpu.roll(first, section, 0), other)
+        return found
+
+    def assembled(parts, quarter):
         total = jnp.zeros((PLANE, LANES), jnp.float32)
         for x in range(4):
-            piece = gathered[pl.ds(8 * x + row, PLANE, stride=32), :]
-            moved = pltpu.roll(piece, 32 * ((x - quarter) % 4), 1) if x != quarter else piece
+            moved = pltpu.roll(parts[x], 32 * ((x - quarter) % 4), 1) if x != quarter else parts[x]
             total = jnp.where(lane // 32 == x, moved, total)
         return total
 
-    def window(rows_quarters):
-        return jnp.concatenate([assembled(r, q) for r, q in rows_quarters], 0)
+    def in_order(own, odd_pair, even_pair):
+        return (jnp.where(even, odd_pair, even_pair), own, jnp.where(even, even_pair, odd_pair))
+
+    def windows(row):
+        parts = [in_order(*[loaded(row + 2 * k)[x] for k in range(3)]) for x in range(4)]
+        join = lambda q: jnp.concatenate([assembled([parts[x][p] for x in range(4)], q) for p in range(3)], 0)
+        return [join(q) for q in range(4)]
 
     def cores_swapped(values):
         even = sublanes_of(WINDOW) % 2 == 0
@@ -199,11 +201,12 @@
     up = lambda v, k: pltpu.roll(v, v.shape[0] - k, 0)
     down = lambda v, k: pltpu.roll(v, k, 0)
 
-    found = [window([(2, q), (0, q), (4, q)]) for q in range(4)]
+    found = windows(0)
     measured = {1: [cores_swapped(found[1]), cores_swapped(found[3])], 2: [found[0], found[2]]}
-    node_links = [window([(3, q), (1, q), (5, q)]).astype(jnp.int32) for q in range(4)]
-    confidence = window([(6, 1), (6, 0), (6, 2)])
-    section = PLANE * (place[0] - 1) + sublanes_of(WINDOW)
+    node_links = [links_of.astype(jnp.int32) for links_of in windows(1)]
+    weights = loaded(6)
+    confidence = jnp.concatenate(in_order(*[assembled(weights, q) for q in range(3)]), 0)
+    section = PLANE * (z - 1) + sublanes_of(WINDOW)
     chain = {d: jnp.where(section >= d, confidence, 0.0) for d, _ in SPRINGS}
 
     first, last = 4, 18
@@ -276,11 +279,11 @@
     line = jnp.sum(jnp.where(lane == sub, totals, 0.0), axis=0, keepdims=True)
     sums_out[...] = jnp.broadcast_to(line[None], sums_out.shape)
 
-    mine = sub == place[1]
+    mine = sub == 2 * y + core
 
     def own(v):
         row = jnp.sum(jnp.where(mine, mid(v), 0.0), axis=0, keepdims=True)
-        return pltpu.roll(row, place[2], 1)
+        return pltpu.roll(row, (LANES - 32 * x_own) % LANES, 1)
 
     fields = [own(f[c]) for f in (start, once, twice) for c in range(2)]
     fields += [own(measured[d][c]) for d in (1, 2) for c in range(2)]
@@ -312,14 +315,12 @@
 
 
 def on_device(pixels, offsets, connections, confidence):
-    z, y, core, x = (lax.axis_index(name) for name in ("z", "y", "core", "x"))
     planes = lax.axis_size("z")
     count = planes * PLANE
     own = pixels[0]
     swap = [(0, 1), (1, 0)]
     prev = lax.ppermute(own, SEC, [(i, i + 2) for i in range(count - 2)])
     f32 = jnp.float32
-    place = jnp.stack([z, 2 * y + core, (LANES - 32 * x) % LANES, core]).astype(jnp.int32)
     held, head, tail, turn, extra = pl.pallas_call(
         prep_kernel,
         out_shape=(
@@ -337,36 +338,40 @@
     ready = pl.pallas_call(
         chip_kernel,
         out_shape=pltpu.VMEM((SUMS, 32, LANES), f32),
-        in_specs=[SMEM] + [VMEM] * 3,
+        in_specs=[VMEM] * 3,
         out_specs=VMEM,
         name="chip",
-    )(place, kept(held), kept(head), kept(tail))
+    )(kept(held), kept(head), kept(tail))
     pay = pl.pallas_call(
         match_kernel,
         out_shape=pltpu.VMEM((8, LANES), f32),
-        in_specs=[SMEM] + [VMEM] * 7,
+        in_specs=[VMEM] * 7,
         out_specs=VMEM,
         scratch_shapes=[pltpu.VMEM((SUMS, 64, LANES), f32)],
         name="match",
-    )(place, *[kept(v) for v in (head, tail, prev, held, turn, ready, extra)])
+    )(*[kept(v) for v in (head, tail, prev, held, turn, ready, extra)])
     swaps = lambda first: [(i + d, i + 1 - d) for i in range(first, planes - 1, 2) for d in (0, 1)]
     odd_pairs = lax.ppermute(pay, "z", swaps(1))
     even_pairs = lax.ppermute(pay, "z", swaps(0))
-    spread = pl.pallas_call(
-        spread_kernel,
-        out_shape=pltpu.VMEM((32, 8, LANES), f32),
-        in_specs=[SMEM] + [VMEM] * 3,
-        out_specs=VMEM,
-        name="spread",
-    )(place, kept(pay), kept(odd_pairs), kept(even_pairs))
-    gathered = lax.all_to_all(spread, ("y", "core", "x"), 0, 0, tiled=True)
+    weights = pay[2:3] + odd_pairs[3:4] + even_pairs[4:5]
+    block = jnp.concatenate([pay[0:2], odd_pairs[0:2], even_pairs[0:2], weights, jnp.zeros((1, LANES), f32)], 0)
+    order = list(range(4 * PLANE))
+    order[0], order[LEADER] = LEADER, 0
+    gathered = lax.all_to_all(
+        jnp.broadcast_to(block, (4 * PLANE, 8, LANES)),
+        ("y", "core", "x"),
+        0,
+        0,
+        tiled=True,
+        axis_index_groups=[order],
+    )
     sums, fields = pl.pallas_call(
         relax_kernel,
         out_shape=(
             pltpu.VMEM((planes, 1, LANES), f32),
             pltpu.VMEM((16, LANES), f32),
         ),
-        in_specs=[SMEM, VMEM],
+        in_specs=[VMEM],
         out_specs=(VMEM, VMEM),
         scratch_shapes=[
             pltpu.VMEM((14, LANES, LANES), jnp.bfloat16),
@@ -374,7 +379,7 @@
             pltpu.VMEM((WINDOW * 8, LANES), f32),
         ],
         name="relax",
-    )(place, kept(gathered.reshape(32 * 8, LANES)))
+    )(kept(gathered.reshape(32 * 8, LANES)))
     turned = [[(i + planes // 2) % planes for i in range(planes)]]
     everywhere = lax.all_to_all(sums, "z", 0, 0, tiled=True, axis_index_groups=turned)
     measured, displacement = pl.pallas_call(

time: 61 us -> 56 us (0.918)
  blocking collectives: 33.9 us -> 30.7 us
  Pallas kernels: 7.56 us -> 4.83 us
  starting transfers between devices: 16.2 us -> 16.9 us
  waiting for transfers between devices: 1.55 us -> 2.2 us
  other arithmetic: 0.66 us -> 0.01 us
    all_to_all x1, blocking collectives: 15.3 us -> 12 us  [on_device(): lax.all_to_all(jnp.broadcast_to(block, (4 * PLANE, 8, LANES)), ('y', 'cor...]
    pallas_call x1 -> x0, Pallas kernels: 0.75 us -> none  [on_device(): pl.pallas_call(spread_kernel, out_shape=pltpu.VMEM((32, 8, LANES), f32),...]
    ppermute x2, waiting for transfers between devices: 0.57 us -> 1.25 us  [on_device(): head, tail = (lax.ppermute(v, 'core', swap) for v in (head, tail))]
    ppermute x1, starting transfers between devices: 3.56 us -> 4.24 us  [on_device(): even_pairs = lax.ppermute(pay, 'z', swaps(0))]
    pallas_call x1, Pallas kernels: 0.67 us -> 0.01 us  [on_device(): pl.pallas_call(chip_kernel, out_shape=pltpu.VMEM((SUMS, 32, LANES), f32),...]
    pallas_call x1, Pallas kernels: 2.39 us -> 1.72 us  [on_device(): pl.pallas_call(match_kernel, out_shape=pltpu.VMEM((8, LANES), f32), in_sp...]
    another operation x1 -> x0, other arithmetic: 0.66 us -> none  [on_device(): jnp.stack([z, 2 * y + core, (LANES - 32 * x) % LANES, core])]
    pallas_call x1, Pallas kernels: 1.95 us -> 1.31 us  [on_device(): pl.pallas_call(relax_kernel, out_shape=(pltpu.VMEM((planes, 1, LANES), f3...]
  transfers between devices with their start and end apart: 5 -> 5, of which waited for: 2 -> 2; matrix products, arithmetic and copies ran while one was open for 1% -> 0% of each run, Pallas kernels for 3% -> 2%
where the time goes in v5:
time: 56 us; the launch traced here: 55.4 us
  blocking collectives  30.7 us (55%)
  starting transfers between devices  16.9 us (30%)
  Pallas kernels  4.83 us (9%)
  waiting for transfers between devices  2.2 us (4%)
  between operations  0.73 us (1%)
    all_to_all x1, blocking collectives, on_device(): lax.all_to_all(sums, 'z', 0, 0, tiled=True, axis_index_groups=turned)  18.7 us
    all_to_all x1, blocking collectives, on_device(): lax.all_to_all(jnp.broadcast_to(block, (4 * PLANE, 8, LANES)), ('y', 'cor...  12 us
    ppermute x2, starting transfers between devices, on_device(): head, tail = (lax.ppermute(v, 'core', swap) for v in (head, tail))  7.97 us
    ppermute x1, starting transfers between devices, on_device(): even_pairs = lax.ppermute(pay, 'z', swaps(0))  4.24 us
    ppermute x1, starting transfers between devices, on_device(): prev = lax.ppermute(own, SEC, [(i, i + 2) for i in range(count - 2)])  4.05 us
    pallas_call x1, Pallas kernels, on_device(): pl.pallas_call(match_kernel, out_shape=pltpu.VMEM((8, LANES), f32), in_sp...  1.72 us
    pallas_call x1, Pallas kernels, on_device(): pl.pallas_call(relax_kernel, out_shape=(pltpu.VMEM((planes, 1, LANES), f3...  1.31 us
    ppermute x2, waiting for transfers between devices, on_device(): head, tail = (lax.ppermute(v, 'core', swap) for v in (head, tail))  1.25 us
  transfers between devices with their start and end apart: 5, of which 2 were waited for; matrix products, arithmetic and copies ran while one was open for 0% of the time, Pallas kernels for 2%

profile of v5, /device:TPU:1, one launch (start us, length us, event | category | flops | bytes accessed | tf_op | source)
XLA Modules:
  0.0 55.4 jit_solution(18239574776417678712)
XLA Ops:
  0.6 4.0 %collective-permute-start.2 = (bf16[32,4096]{1,0:T(8,128)(2,1)}, bf16[32,4096]{1,0:T(8,128)(2,1)S(1)}, u32[]{:S(2)}, u32[]{:S(2)}) collective-permute-start(bf16[32,4096]{1,0:T(8,128)(2,1)} %bitcast.3), channel_id=1, source_target_pairs={{0,8},{4,12},{8,16},{12,20},{16,24},{20,28},{24,32},{28,36},{32,40... | collective-permute-start | bytes 786440 | tf_op jit(solution)/shard_map/ppermute | solution.py:322
  4.7 1.1 %prep.1 = (bf16[32,4096]{1,0:T(8,128)(2,1)S(1)}, bf16[32,3072]{1,0:T(8,128)(2,1)S(1)}, bf16[32,1280]{1,0:T(8,128)(2,1)S(1)}, s32[64,128]{1,0:T(8,128)S(1)}, f32[8,128]{1,0:T(8,128)S(1)}) custom-call(bf16[32,4096]{1,0:T(8,128)(2,1)} %bitcast.4, s32[2,2,1,32]{3,2,1,0:T(1,128)} %offsets.1, s32[4,1,32]{2,1,0:T(1,128)} %connections.1, f32[1,32]{1,0:T(1,128)} %confidence.1), custom_call_target="tpu_custom_call" | custom-call | tf_op jit(solution)/shard_map/prep/pallas_call | solution.py:324
  5.8 6.0 %collective-permute-start = (bf16[32,3072]{1,0:T(8,128)(2,1)S(1)}, bf16[32,3072]{1,0:T(8,128)(2,1)S(1)}, u32[]{:S(2)}, u32[]{:S(2)}) collective-permute-start(bf16[32,3072]{1,0:T(8,128)(2,1)S(1)} %get-tuple-element.9), channel_id=1, source_target_pairs={{0,4},{4,0},{1,5},{5,1},{2,6},{6,2},{3,7},{7,3},{8,12},{12,8},{9,1... | collective-permute-start | bytes 589832 | tf_op jit(solution)/shard_map/ppermute | solution.py:337
  11.8 1.9 %collective-permute-start.1 = (bf16[32,1280]{1,0:T(8,128)(2,1)S(1)}, bf16[32,1280]{1,0:T(8,128)(2,1)S(1)}, u32[]{:S(2)}, u32[]{:S(2)}) collective-permute-start(bf16[32,1280]{1,0:T(8,128)(2,1)S(1)} %get-tuple-element.10), channel_id=1, source_target_pairs={{0,4},{4,0},{1,5},{5,1},{2,6},{6,2},{3,7},{7,3},{8,12},{12,8},{9,1... | collective-permute-start | bytes 245768 | tf_op jit(solution)/shard_map/ppermute | solution.py:337
  13.8 1.2 %collective-permute-done.1.tail = bf16[32,1280]{1,0:T(8,128)(2,1)S(1)} collective-permute-done((bf16[32,1280]{1,0:T(8,128)(2,1)S(1)}, bf16[32,1280]{1,0:T(8,128)(2,1)S(1)}, u32[]{:S(2)}, u32[]{:S(2)}) %collective-permute-start.1) | collective-permute-done | bytes 81952 | tf_op jit(solution)/shard_map/ppermute | solution.py:337
  15.0 0.0 collective-permute-done.head
  15.0 0.0 collective-permute-done.2.prev
  15.0 1.7 %match.1 = f32[8,128]{1,0:T(8,128)S(1)} custom-call(bf16[32,3072]{1,0:T(8,128)(2,1)S(1)} %collective-permute-done.head, bf16[32,1280]{1,0:T(8,128)(2,1)S(1)} %collective-permute-done.1.tail, bf16[32,4096]{1,0:T(8,128)(2,1)S(1)} %collective-permute-done.2.prev, bf16[32,4096]{1,0:T(8,128)(2,1)S(1)} %get-tuple-element.11.own, ...), custom_call_target="tpu_custom_call" | custom-call | tf_op jit(solution)/shard_map/match/pallas_call | solution.py:345
  16.8 0.7 %collective-permute-start.3 = (f32[8,128]{1,0:T(8,128)S(1)}, f32[8,128]{1,0:T(8,128)S(1)}, u32[]{:S(2)}, u32[]{:S(2)}) collective-permute-start(f32[8,128]{1,0:T(8,128)S(1)} %match.1), channel_id=1, source_target_pairs={{32,64},{64,32},{96,128},{128,96},{160,192},{192,160},{224,256},{2... | collective-permute-start | bytes 12296 | tf_op jit(solution)/shard_map/ppermute | solution.py:354
  17.4 4.2 %collective-permute-start.4 = (f32[8,128]{1,0:T(8,128)S(1)}, f32[8,128]{1,0:T(8,128)S(1)}, u32[]{:S(2)}, u32[]{:S(2)}) collective-permute-start(f32[8,128]{1,0:T(8,128)S(1)} %match.1), channel_id=1, source_target_pairs={{0,32},{32,0},{64,96},{96,64},{128,160},{160,128},{192,224},{224,1... | collective-permute-start | bytes 12296 | tf_op jit(solution)/shard_map/ppermute | solution.py:355
  21.7 0.0 collective-permute-done.3
  21.7 0.9 %collective-permute-done.4 = f32[8,128]{1,0:T(8,128)S(1)} collective-permute-done((f32[8,128]{1,0:T(8,128)S(1)}, f32[8,128]{1,0:T(8,128)S(1)}, u32[]{:S(2)}, u32[]{:S(2)}) %collective-permute-start.4) | collective-permute-done | bytes 4128 | tf_op jit(solution)/shard_map/ppermute | solution.py:355
  22.7 12.0 %all_to_all.10 = f32[32,8,128]{2,1,0:T(8,128)S(1)} all-to-all(f32[32,8,128]{2,1,0:T(8,128)S(1)} %broadcast_in_dim.7), channel_id=1, replica_groups={{22,1,2,3,4,5,6,7,8,9,10,11,12,13,14,15,16,17,18,19,20,21,0,23,24,25,26..., dimensions={0} | all-to-all | bytes 262144 | tf_op jit(solution)/shard_map/all_to_all | solution.py:360
  34.7 1.3 %relax.1 = (f32[16,1,128]{2,1,0:T(1,128)S(1)}, f32[16,128]{1,0:T(8,128)S(1)}) custom-call(f32[256,128]{1,0:T(8,128)S(1)} %bitcast.2), custom_call_target="tpu_custom_call" | custom-call | tf_op jit(solution)/shard_map/relax/pallas_call | solution.py:368
  36.0 18.7 %all_to_all.11.sums = f32[16,1,128]{2,1,0:T(1,128)S(1)} all-to-all(f32[16,1,128]{2,1,0:T(1,128)S(1)} %get-tuple-element.14), channel_id=1, replica_groups={{256,288,320,352,384,416,448,480,0,32,64,96,128,160,192,224},{257,289,3..., dimensions={0} | all-to-all | bytes 16384 | tf_op jit(solution)/shard_map/all_to_all | solution.py:384
  54.7 0.7 %finish.1 = (f32[2,2,1,32]{3,2,1,0:T(1,128)}, f32[2,1,32]{2,1,0:T(1,128)}) custom-call(f32[16,1,128]{2,1,0:T(1,128)S(1)} %all_to_all.11.sums, f32[16,128]{1,0:T(8,128)S(1)} %get-tuple-element.15.fields), custom_call_target="tpu_custom_call" | custom-call | tf_op jit(solution)/shard_map/finish/pallas_call | solution.py:385
  (8 shorter events, 0.1 us)
Async XLA Ops:
  0.6 14.4 %collective-permute-start.2 = (bf16[32,4096]{1,0:T(8,128)(2,1)}, bf16[32,4096]{1,0:T(8,128)(2,1)S(1)}, u32[]{:S(2)}, u32[]{:S(2)}) collective-permute-start(bf16[32,4096]{1,0:T(8,128)(2,1)} %bitcast.3), channel_id=1, source_target_pairs={{0,8},{4,12},{8,16},{12,20},{16,24},{20,28},{24,32},{28,36},{32,40... | collective-permute-start | bytes 786440 | tf_op jit(solution)/shard_map/ppermute | solution.py:322
  5.8 9.2 %collective-permute-start = (bf16[32,3072]{1,0:T(8,128)(2,1)S(1)}, bf16[32,3072]{1,0:T(8,128)(2,1)S(1)}, u32[]{:S(2)}, u32[]{:S(2)}) collective-permute-start(bf16[32,3072]{1,0:T(8,128)(2,1)S(1)} %get-tuple-element.9), channel_id=1, source_target_pairs={{0,4},{4,0},{1,5},{5,1},{2,6},{6,2},{3,7},{7,3},{8,12},{12,8},{9,1... | collective-permute-start | bytes 589832 | tf_op jit(solution)/shard_map/ppermute | solution.py:337
  11.8 3.2 %collective-permute-start.1 = (bf16[32,1280]{1,0:T(8,128)(2,1)S(1)}, bf16[32,1280]{1,0:T(8,128)(2,1)S(1)}, u32[]{:S(2)}, u32[]{:S(2)}) collective-permute-start(bf16[32,1280]{1,0:T(8,128)(2,1)S(1)} %get-tuple-element.10), channel_id=1, source_target_pairs={{0,4},{4,0},{1,5},{5,1},{2,6},{6,2},{3,7},{7,3},{8,12},{12,8},{9,1... | collective-permute-start | bytes 245768 | tf_op jit(solution)/shard_map/ppermute | solution.py:337
  16.8 4.9 %collective-permute-start.3 = (f32[8,128]{1,0:T(8,128)S(1)}, f32[8,128]{1,0:T(8,128)S(1)}, u32[]{:S(2)}, u32[]{:S(2)}) collective-permute-start(f32[8,128]{1,0:T(8,128)S(1)} %match.1), channel_id=1, source_target_pairs={{32,64},{64,32},{96,128},{128,96},{160,192},{192,160},{224,256},{2... | collective-permute-start | bytes 12296 | tf_op jit(solution)/shard_map/ppermute | solution.py:354
  17.4 5.2 %collective-permute-start.4 = (f32[8,128]{1,0:T(8,128)S(1)}, f32[8,128]{1,0:T(8,128)S(1)}, u32[]{:S(2)}, u32[]{:S(2)}) collective-permute-start(f32[8,128]{1,0:T(8,128)S(1)} %match.1), channel_id=1, source_target_pairs={{0,32},{32,0},{64,96},{96,64},{128,160},{160,128},{192,224},{224,1... | collective-permute-start | bytes 12296 | tf_op jit(solution)/shard_map/ppermute | solution.py:355

commit v6 on v5

--- a/solution.py
+++ b/solution.py
@@ -380,8 +380,10 @@
         ],
         name="relax",
     )(kept(gathered.reshape(32 * 8, LANES)))
-    turned = [[(i + planes // 2) % planes for i in range(planes)]]
-    everywhere = lax.all_to_all(sums, "z", 0, 0, tiled=True, axis_index_groups=turned)
+    far = range(planes // 4, 3 * planes // 4)
+    turned = [(i + planes // 2) % planes for i in range(planes)]
+    mixed = [[2 * i + (1 - core if i in far else core) for i in turned] for core in (0, 1)]
+    everywhere = lax.all_to_all(sums, ("z", "core"), 0, 0, tiled=True, axis_index_groups=mixed)
     measured, displacement = pl.pallas_call(
         finish_kernel,
         out_shape=(jax.ShapeDtypeStruct((2, 2, 1, 32), f32), jax.ShapeDtypeStruct((2, 1, 32), f32)),

time: 56 us -> 56.7 us (1.012)
  blocking collectives: 30.7 us -> 31.7 us
    all_to_all x1, blocking collectives: 18.7 us -> 19.7 us  [on_device(): lax.all_to_all(sums, ('z', 'core'), 0, 0, tiled=True, axis_index_groups=m...]
where the time goes in v6:
time: 56.7 us; the launch traced here: 56.4 us
  blocking collectives  31.7 us (56%)
  starting transfers between devices  16.9 us (30%)
  Pallas kernels  4.83 us (9%)
  waiting for transfers between devices  2.2 us (4%)
  between operations  0.73 us (1%)
    all_to_all x1, blocking collectives, on_device(): lax.all_to_all(sums, ('z', 'core'), 0, 0, tiled=True, axis_index_groups=m...  19.7 us
    all_to_all x1, blocking collectives, on_device(): lax.all_to_all(jnp.broadcast_to(block, (4 * PLANE, 8, LANES)), ('y', 'cor...  12 us
    ppermute x2, starting transfers between devices, on_device(): head, tail = (lax.ppermute(v, 'core', swap) for v in (head, tail))  7.97 us
    ppermute x1, starting transfers between devices, on_device(): even_pairs = lax.ppermute(pay, 'z', swaps(0))  4.24 us
    ppermute x1, starting transfers between devices, on_device(): prev = lax.ppermute(own, SEC, [(i, i + 2) for i in range(count - 2)])  4.05 us
    pallas_call x1, Pallas kernels, on_device(): pl.pallas_call(match_kernel, out_shape=pltpu.VMEM((8, LANES), f32), in_sp...  1.72 us
    pallas_call x1, Pallas kernels, on_device(): pl.pallas_call(relax_kernel, out_shape=(pltpu.VMEM((planes, 1, LANES), f3...  1.31 us
    ppermute x2, waiting for transfers between devices, on_device(): head, tail = (lax.ppermute(v, 'core', swap) for v in (head, tail))  1.25 us
  transfers between devices with their start and end apart: 5, of which 2 were waited for; matrix products, arithmetic and copies ran while one was open for 0% of the time, Pallas kernels for 2%

profile of v6, /device:TPU:1, one launch (start us, length us, event | category | flops | bytes accessed | tf_op | source)
XLA Modules:
  0.0 56.4 jit_solution(15871930575101168683)
XLA Ops:
  0.6 4.0 %collective-permute-start.2 = (bf16[32,4096]{1,0:T(8,128)(2,1)}, bf16[32,4096]{1,0:T(8,128)(2,1)S(1)}, u32[]{:S(2)}, u32[]{:S(2)}) collective-permute-start(bf16[32,4096]{1,0:T(8,128)(2,1)} %bitcast.3), channel_id=1, source_target_pairs={{0,8},{4,12},{8,16},{12,20},{16,24},{20,28},{24,32},{28,36},{32,40... | collective-permute-start | bytes 786440 | tf_op jit(solution)/shard_map/ppermute | solution.py:322
  4.7 1.1 %prep.1 = (bf16[32,4096]{1,0:T(8,128)(2,1)S(1)}, bf16[32,3072]{1,0:T(8,128)(2,1)S(1)}, bf16[32,1280]{1,0:T(8,128)(2,1)S(1)}, s32[64,128]{1,0:T(8,128)S(1)}, f32[8,128]{1,0:T(8,128)S(1)}) custom-call(bf16[32,4096]{1,0:T(8,128)(2,1)} %bitcast.4, s32[2,2,1,32]{3,2,1,0:T(1,128)} %offsets.1, s32[4,1,32]{2,1,0:T(1,128)} %connections.1, f32[1,32]{1,0:T(1,128)} %confidence.1), custom_call_target="tpu_custom_call" | custom-call | tf_op jit(solution)/shard_map/prep/pallas_call | solution.py:324
  5.8 6.0 %collective-permute-start = (bf16[32,3072]{1,0:T(8,128)(2,1)S(1)}, bf16[32,3072]{1,0:T(8,128)(2,1)S(1)}, u32[]{:S(2)}, u32[]{:S(2)}) collective-permute-start(bf16[32,3072]{1,0:T(8,128)(2,1)S(1)} %get-tuple-element.9), channel_id=1, source_target_pairs={{0,4},{4,0},{1,5},{5,1},{2,6},{6,2},{3,7},{7,3},{8,12},{12,8},{9,1... | collective-permute-start | bytes 589832 | tf_op jit(solution)/shard_map/ppermute | solution.py:337
  11.8 1.9 %collective-permute-start.1 = (bf16[32,1280]{1,0:T(8,128)(2,1)S(1)}, bf16[32,1280]{1,0:T(8,128)(2,1)S(1)}, u32[]{:S(2)}, u32[]{:S(2)}) collective-permute-start(bf16[32,1280]{1,0:T(8,128)(2,1)S(1)} %get-tuple-element.10), channel_id=1, source_target_pairs={{0,4},{4,0},{1,5},{5,1},{2,6},{6,2},{3,7},{7,3},{8,12},{12,8},{9,1... | collective-permute-start | bytes 245768 | tf_op jit(solution)/shard_map/ppermute | solution.py:337
  13.8 1.2 %collective-permute-done.1.tail = bf16[32,1280]{1,0:T(8,128)(2,1)S(1)} collective-permute-done((bf16[32,1280]{1,0:T(8,128)(2,1)S(1)}, bf16[32,1280]{1,0:T(8,128)(2,1)S(1)}, u32[]{:S(2)}, u32[]{:S(2)}) %collective-permute-start.1) | collective-permute-done | bytes 81952 | tf_op jit(solution)/shard_map/ppermute | solution.py:337
  15.0 0.0 collective-permute-done.head
  15.0 0.0 collective-permute-done.2.prev
  15.0 1.7 %match.1 = f32[8,128]{1,0:T(8,128)S(1)} custom-call(bf16[32,3072]{1,0:T(8,128)(2,1)S(1)} %collective-permute-done.head, bf16[32,1280]{1,0:T(8,128)(2,1)S(1)} %collective-permute-done.1.tail, bf16[32,4096]{1,0:T(8,128)(2,1)S(1)} %collective-permute-done.2.prev, bf16[32,4096]{1,0:T(8,128)(2,1)S(1)} %get-tuple-element.11.own, ...), custom_call_target="tpu_custom_call" | custom-call | tf_op jit(solution)/shard_map/match/pallas_call | solution.py:345
  16.8 0.7 %collective-permute-start.3 = (f32[8,128]{1,0:T(8,128)S(1)}, f32[8,128]{1,0:T(8,128)S(1)}, u32[]{:S(2)}, u32[]{:S(2)}) collective-permute-start(f32[8,128]{1,0:T(8,128)S(1)} %match.1), channel_id=1, source_target_pairs={{32,64},{64,32},{96,128},{128,96},{160,192},{192,160},{224,256},{2... | collective-permute-start | bytes 12296 | tf_op jit(solution)/shard_map/ppermute | solution.py:354
  17.4 4.2 %collective-permute-start.4 = (f32[8,128]{1,0:T(8,128)S(1)}, f32[8,128]{1,0:T(8,128)S(1)}, u32[]{:S(2)}, u32[]{:S(2)}) collective-permute-start(f32[8,128]{1,0:T(8,128)S(1)} %match.1), channel_id=1, source_target_pairs={{0,32},{32,0},{64,96},{96,64},{128,160},{160,128},{192,224},{224,1... | collective-permute-start | bytes 12296 | tf_op jit(solution)/shard_map/ppermute | solution.py:355
  21.7 0.0 collective-permute-done.3
  21.7 0.9 %collective-permute-done.4 = f32[8,128]{1,0:T(8,128)S(1)} collective-permute-done((f32[8,128]{1,0:T(8,128)S(1)}, f32[8,128]{1,0:T(8,128)S(1)}, u32[]{:S(2)}, u32[]{:S(2)}) %collective-permute-start.4) | collective-permute-done | bytes 4128 | tf_op jit(solution)/shard_map/ppermute | solution.py:355
  22.7 12.0 %all_to_all.10 = f32[32,8,128]{2,1,0:T(8,128)S(1)} all-to-all(f32[32,8,128]{2,1,0:T(8,128)S(1)} %broadcast_in_dim.7), channel_id=1, replica_groups={{22,1,2,3,4,5,6,7,8,9,10,11,12,13,14,15,16,17,18,19,20,21,0,23,24,25,26..., dimensions={0} | all-to-all | bytes 262144 | tf_op jit(solution)/shard_map/all_to_all | solution.py:360
  34.7 1.3 %relax.1 = (f32[16,1,128]{2,1,0:T(1,128)S(1)}, f32[16,128]{1,0:T(8,128)S(1)}) custom-call(f32[256,128]{1,0:T(8,128)S(1)} %bitcast.2), custom_call_target="tpu_custom_call" | custom-call | tf_op jit(solution)/shard_map/relax/pallas_call | solution.py:368
  36.0 19.7 %all_to_all.11.sums = f32[16,1,128]{2,1,0:T(1,128)S(1)} all-to-all(f32[16,1,128]{2,1,0:T(1,128)S(1)} %get-tuple-element.14), channel_id=1, replica_groups={{260,292,324,356,384,416,448,480,0,32,64,96,132,164,196,228},{256,288,3..., dimensions={0} | all-to-all | bytes 16384 | tf_op jit(solution)/shard_map/all_to_all | solution.py:386
  55.7 0.7 %finish.1 = (f32[2,2,1,32]{3,2,1,0:T(1,128)}, f32[2,1,32]{2,1,0:T(1,128)}) custom-call(f32[16,1,128]{2,1,0:T(1,128)S(1)} %all_to_all.11.sums, f32[16,128]{1,0:T(8,128)S(1)} %get-tuple-element.15.fields), custom_call_target="tpu_custom_call" | custom-call | tf_op jit(solution)/shard_map/finish/pallas_call | solution.py:387
  (8 shorter events, 0.1 us)
Async XLA Ops:
  0.6 14.4 %collective-permute-start.2 = (bf16[32,4096]{1,0:T(8,128)(2,1)}, bf16[32,4096]{1,0:T(8,128)(2,1)S(1)}, u32[]{:S(2)}, u32[]{:S(2)}) collective-permute-start(bf16[32,4096]{1,0:T(8,128)(2,1)} %bitcast.3), channel_id=1, source_target_pairs={{0,8},{4,12},{8,16},{12,20},{16,24},{20,28},{24,32},{28,36},{32,40... | collective-permute-start | bytes 786440 | tf_op jit(solution)/shard_map/ppermute | solution.py:322
  5.8 9.2 %collective-permute-start = (bf16[32,3072]{1,0:T(8,128)(2,1)S(1)}, bf16[32,3072]{1,0:T(8,128)(2,1)S(1)}, u32[]{:S(2)}, u32[]{:S(2)}) collective-permute-start(bf16[32,3072]{1,0:T(8,128)(2,1)S(1)} %get-tuple-element.9), channel_id=1, source_target_pairs={{0,4},{4,0},{1,5},{5,1},{2,6},{6,2},{3,7},{7,3},{8,12},{12,8},{9,1... | collective-permute-start | bytes 589832 | tf_op jit(solution)/shard_map/ppermute | solution.py:337
  11.8 3.2 %collective-permute-start.1 = (bf16[32,1280]{1,0:T(8,128)(2,1)S(1)}, bf16[32,1280]{1,0:T(8,128)(2,1)S(1)}, u32[]{:S(2)}, u32[]{:S(2)}) collective-permute-start(bf16[32,1280]{1,0:T(8,128)(2,1)S(1)} %get-tuple-element.10), channel_id=1, source_target_pairs={{0,4},{4,0},{1,5},{5,1},{2,6},{6,2},{3,7},{7,3},{8,12},{12,8},{9,1... | collective-permute-start | bytes 245768 | tf_op jit(solution)/shard_map/ppermute | solution.py:337
  16.8 4.9 %collective-permute-start.3 = (f32[8,128]{1,0:T(8,128)S(1)}, f32[8,128]{1,0:T(8,128)S(1)}, u32[]{:S(2)}, u32[]{:S(2)}) collective-permute-start(f32[8,128]{1,0:T(8,128)S(1)} %match.1), channel_id=1, source_target_pairs={{32,64},{64,32},{96,128},{128,96},{160,192},{192,160},{224,256},{2... | collective-permute-start | bytes 12296 | tf_op jit(solution)/shard_map/ppermute | solution.py:354
  17.4 5.2 %collective-permute-start.4 = (f32[8,128]{1,0:T(8,128)S(1)}, f32[8,128]{1,0:T(8,128)S(1)}, u32[]{:S(2)}, u32[]{:S(2)}) collective-permute-start(f32[8,128]{1,0:T(8,128)S(1)} %match.1), channel_id=1, source_target_pairs={{0,32},{32,0},{64,96},{96,64},{128,160},{160,128},{192,224},{224,1... | collective-permute-start | bytes 12296 | tf_op jit(solution)/shard_map/ppermute | solution.py:355

commit v7 on v5

--- a/solution.py
+++ b/solution.py
@@ -53,24 +53,36 @@
     return [jnp.where(odd_high, tiles[j - 1], tiles[j]) for j in range(TILES)]
 
 
-def products(a_tile, b_tile, shift_rows, shift_cols):
+def rows_around(tile_of):
+    low = lanes_of(ROWS) < PIX
+    known = {}
+
+    def rolled(j):
+        j %= TILES
+        if j not in known:
+            known[j] = pltpu.roll(tile_of(j), PIX, 1)
+        return known[j]
+
+    return lambda j: (
+        jnp.where(low, rolled(j - 1), rolled(j)),
+        tile_of(j),
+        jnp.where(low, rolled(j), rolled(j + 1)),
+    )
+
+
+def products(around, b_tile, shift_rows, shift_cols):
     lane = lanes_of(ROWS)
-    low = lane < PIX
     moved = shifted_tiles(b_tile, shift_rows, lane)
     half = (lane ^ (PIX * (shift_rows & 1))) & PIX
     index = [half | ((lane - shift_cols - e) & (PIX - 1)) for e in (-1, 0, 1)]
-    rolled = lambda j: pltpu.roll(a_tile(j % TILES), PIX, 1)
     sums = [jnp.zeros((ROWS, LANES), jnp.float32)] * SUMS
-    before, here = rolled(TILES - 1), rolled(0)
     for j in range(TILES):
-        after = rolled(j + 1)
-        centre = a_tile(j)
-        rows_a = (jnp.where(low, before, here), centre, jnp.where(low, here, after))
+        rows_a = around(j)
+        centre = rows_a[1]
         cols_b = [pick_rows(moved[j], index[e]) for e in range(3)]
         terms = [rows_a[e1] * cols_b[e2] for e1 in range(3) for e2 in range(3)]
         terms += [centre * centre, cols_b[1] * cols_b[1]]
         sums = [total + term for total, term in zip(sums, terms)]
-        before, here = here, after
     return sums
 
 
@@ -84,10 +96,14 @@
     return tile
 
 
-def pair_products(out, at, a_refs, b_refs, turn):
+def pair_products(out, at, a_refs, b_refs, turn, faces=None):
     for g in range(2):
         rows = slice(ROWS * g, ROWS * (g + 1))
-        sums = products(tile_reader(a_refs, g), tile_reader(b_refs, g), turn(0, rows), turn(1, rows))
+        if faces is None:
+            around = rows_around(tile_reader(a_refs, g))
+        else:
+            around = lambda j, rows=rows: [faces[e, rows, LANES * j : LANES * (j + 1)] for e in range(3)]
+        sums = products(around, tile_reader(b_refs, g), turn(0, rows), turn(1, rows))
         for k in range(SUMS):
             out[k, at + ROWS * g : at + ROWS * (g + 1), :] = sums[k]
 
@@ -126,13 +142,19 @@
         extra[2 + k : 3 + k, 32 * k : 32 * (k + 1)] = confidence[...]
 
 
-def chip_kernel(own, head, tail, ready):
+def chip_kernel(own, head, tail, ready, faces):
+    for g in range(2):
+        around = rows_around(tile_reader((own,), g))
+        for j in range(TILES):
+            for e, face in enumerate(around(j)):
+                faces[e, ROWS * g : ROWS * (g + 1), LANES * j : LANES * (j + 1)] = face
+
     @pl.when(lax.axis_index("core") == 0)
     def _():
         pair_products(ready, 0, (head, tail), (own,), sent_turns(tail))
 
 
-def match_kernel(head, tail, prev, own, turn, ready, extra, pay, sums):
+def match_kernel(head, tail, prev, faces, turn, ready, extra, pay, sums):
     core = lax.axis_index("core")
 
     @pl.when(core == 0)
@@ -143,7 +165,7 @@
     def _():
         pair_products(sums, 32, (head, tail), (prev,), sent_turns(tail))
 
-    pair_products(sums, 0, (own,), (prev,), own_turns(turn))
+    pair_products(sums, 0, None, (prev,), own_turns(turn), faces)
     total = [jnp.sum(sums[k], axis=1, keepdims=True) for k in range(SUMS)]
     scale = (total[9] / PIX**2 + 1e-05) * (total[10] / PIX**2 + 1e-05) * PIX**2
     inverse = 1.0 / scale
@@ -335,11 +357,11 @@
         name="prep",
     )(own, offsets, connections, confidence)
     head, tail = (lax.ppermute(v, "core", swap) for v in (head, tail))
-    ready = pl.pallas_call(
+    ready, faces = pl.pallas_call(
         chip_kernel,
-        out_shape=pltpu.VMEM((SUMS, 32, LANES), f32),
+        out_shape=(pltpu.VMEM((SUMS, 32, LANES), f32), pltpu.VMEM((3, 32, PIX * PIX), f32)),
         in_specs=[VMEM] * 3,
-        out_specs=VMEM,
+        out_specs=(VMEM, VMEM),
         name="chip",
     )(kept(held), kept(head), kept(tail))
     pay = pl.pallas_call(
@@ -349,7 +371,7 @@
         out_specs=VMEM,
         scratch_shapes=[pltpu.VMEM((SUMS, 64, LANES), f32)],
         name="match",
-    )(*[kept(v) for v in (head, tail, prev, held, turn, ready, extra)])
+    )(*[kept(v) for v in (head, tail, prev, faces, turn, ready, extra)])
     swaps = lambda first: [(i + d, i + 1 - d) for i in range(first, planes - 1, 2) for d in (0, 1)]
     odd_pairs = lax.ppermute(pay, "z", swaps(1))
     even_pairs = lax.ppermute(pay, "z", swaps(0))

time: 56 us -> 57.3 us (1.023)
  local copies, waits for them, and re-layouts: 0.05 us -> 2.59 us
  starting transfers between devices: 16.9 us -> 15.9 us
    unnamed x0 -> x4, local copies, waits for them, and re-layouts: none -> 2.55 us
    ppermute x1, starting transfers between devices: 4.24 us -> 3.25 us  [on_device(): even_pairs = lax.ppermute(pay, 'z', swaps(0))]
    all_to_all x1, blocking collectives: 18.7 us -> 18.1 us  [on_device(): lax.all_to_all(sums, 'z', 0, 0, tiled=True, axis_index_groups=turned)]
where the time goes in v7:
time: 57.3 us; the launch traced here: 56.7 us
  blocking collectives  30.2 us (53%)
  starting transfers between devices  15.9 us (28%)
  Pallas kernels  4.89 us (9%)
  local copies, waits for them, and re-layouts  2.59 us (5%)
  waiting for transfers between devices  2.32 us (4%)
  between operations  0.75 us (1%)
    all_to_all x1, blocking collectives, on_device(): lax.all_to_all(sums, 'z', 0, 0, tiled=True, axis_index_groups=turned)  18.1 us
    all_to_all x1, blocking collectives, on_device(): lax.all_to_all(jnp.broadcast_to(block, (4 * PLANE, 8, LANES)), ('y', 'cor...  12.2 us
    ppermute x2, starting transfers between devices, on_device(): head, tail = (lax.ppermute(v, 'core', swap) for v in (head, tail))  7.97 us
    ppermute x1, starting transfers between devices, on_device(): prev = lax.ppermute(own, SEC, [(i, i + 2) for i in range(count - 2)])  4.05 us
    ppermute x1, starting transfers between devices, on_device(): even_pairs = lax.ppermute(pay, 'z', swaps(0))  3.25 us
    unnamed x4, local copies, waits for them, and re-layouts  2.55 us
    pallas_call x1, Pallas kernels, on_device(): pl.pallas_call(match_kernel, out_shape=pltpu.VMEM((8, LANES), f32), in_sp...  1.63 us
    pallas_call x1, Pallas kernels, on_device(): pl.pallas_call(relax_kernel, out_shape=(pltpu.VMEM((planes, 1, LANES), f3...  1.31 us
  transfers between devices with their start and end apart: 5, of which 2 were waited for; matrix products, arithmetic and copies ran while one was open for 0% of the time, Pallas kernels for 2%

profile of v7, /device:TPU:1, one launch (start us, length us, event | category | flops | bytes accessed | tf_op | source)
XLA Modules:
  0.0 56.7 jit_solution(10019294797163959038)
XLA Ops:
  0.6 4.0 %collective-permute-start.2 = (bf16[32,4096]{1,0:T(8,128)(2,1)}, bf16[32,4096]{1,0:T(8,128)(2,1)S(1)}, u32[]{:S(2)}, u32[]{:S(2)}) collective-permute-start(bf16[32,4096]{1,0:T(8,128)(2,1)} %bitcast.3), channel_id=1, source_target_pairs={{0,8},{4,12},{8,16},{12,20},{16,24},{20,28},{24,32},{28,36},{32,40... | collective-permute-start | bytes 786440 | tf_op jit(solution)/shard_map/ppermute | solution.py:344
  4.7 1.1 %prep.1 = (bf16[32,4096]{1,0:T(8,128)(2,1)S(1)}, bf16[32,3072]{1,0:T(8,128)(2,1)S(1)}, bf16[32,1280]{1,0:T(8,128)(2,1)S(1)}, s32[64,128]{1,0:T(8,128)S(1)}, f32[8,128]{1,0:T(8,128)S(1)}) custom-call(bf16[32,4096]{1,0:T(8,128)(2,1)} %bitcast.4, s32[2,2,1,32]{3,2,1,0:T(1,128)} %offsets.1, s32[4,1,32]{2,1,0:T(1,128)} %connections.1, f32[1,32]{1,0:T(1,128)} %confidence.1), custom_call_target="tpu_custom_call" | custom-call | tf_op jit(solution)/shard_map/prep/pallas_call | solution.py:346
  5.8 6.0 %collective-permute-start = (bf16[32,3072]{1,0:T(8,128)(2,1)S(1)}, bf16[32,3072]{1,0:T(8,128)(2,1)S(1)}, u32[]{:S(2)}, u32[]{:S(2)}) collective-permute-start(bf16[32,3072]{1,0:T(8,128)(2,1)S(1)} %get-tuple-element.11), channel_id=1, source_target_pairs={{0,4},{4,0},{1,5},{5,1},{2,6},{6,2},{3,7},{7,3},{8,12},{12,8},{9,1... | collective-permute-start | bytes 589832 | tf_op jit(solution)/shard_map/ppermute | solution.py:359
  11.8 1.9 %collective-permute-start.1 = (bf16[32,1280]{1,0:T(8,128)(2,1)S(1)}, bf16[32,1280]{1,0:T(8,128)(2,1)S(1)}, u32[]{:S(2)}, u32[]{:S(2)}) collective-permute-start(bf16[32,1280]{1,0:T(8,128)(2,1)S(1)} %get-tuple-element.12), channel_id=1, source_target_pairs={{0,4},{4,0},{1,5},{5,1},{2,6},{6,2},{3,7},{7,3},{8,12},{12,8},{9,1... | collective-permute-start | bytes 245768 | tf_op jit(solution)/shard_map/ppermute | solution.py:359
  13.8 1.2 %collective-permute-done.1.tail = bf16[32,1280]{1,0:T(8,128)(2,1)S(1)} collective-permute-done((bf16[32,1280]{1,0:T(8,128)(2,1)S(1)}, bf16[32,1280]{1,0:T(8,128)(2,1)S(1)}, u32[]{:S(2)}, u32[]{:S(2)}) %collective-permute-start.1) | collective-permute-done | bytes 81952 | tf_op jit(solution)/shard_map/ppermute | solution.py:359
  15.0 0.0 collective-permute-done.head
  15.0 0.1 chip.1
  15.2 0.0 copy-start
  15.2 1.1 %copy-done = f32[3,32,4096]{2,1,0:T(8,128)} copy-done((f32[3,32,4096]{2,1,0:T(8,128)}, f32[3,32,4096]{2,1,0:T(8,128)S(1)}, u32[]{:S(2)}) %copy-start) | copy-done | bytes 1572888
  16.3 0.0 collective-permute-done.2.prev
  16.3 0.0 copy-start.1
  16.3 1.4 %copy-done.1 = f32[3,32,4096]{2,1,0:T(8,128)S(1)} copy-done((f32[3,32,4096]{2,1,0:T(8,128)S(1)}, f32[3,32,4096]{2,1,0:T(8,128)}, u32[]{:S(2)}) %copy-start.1) | copy-done | bytes 1572888
  17.7 1.6 %match.1 = f32[8,128]{1,0:T(8,128)S(1)} custom-call(bf16[32,3072]{1,0:T(8,128)(2,1)S(1)} %collective-permute-done.head, bf16[32,1280]{1,0:T(8,128)(2,1)S(1)} %collective-permute-done.1.tail, bf16[32,4096]{1,0:T(8,128)(2,1)S(1)} %collective-permute-done.2.prev, f32[3,32,4096]{2,1,0:T(8,128)S(1)} %copy-done.1, s32[64,128]{1,0:T(8,128)S(1)} %get-tuple-element.15.turn, ...), custom_call_target="tpu_custom_call" | custom-call | tf_op jit(solution)/shard_map/match/pallas_call | solution.py:367
  19.4 0.7 %collective-permute-start.3 = (f32[8,128]{1,0:T(8,128)S(1)}, f32[8,128]{1,0:T(8,128)S(1)}, u32[]{:S(2)}, u32[]{:S(2)}) collective-permute-start(f32[8,128]{1,0:T(8,128)S(1)} %match.1), channel_id=1, source_target_pairs={{32,64},{64,32},{96,128},{128,96},{160,192},{192,160},{224,256},{2... | collective-permute-start | bytes 12296 | tf_op jit(solution)/shard_map/ppermute | solution.py:376
  20.0 3.2 %collective-permute-start.4 = (f32[8,128]{1,0:T(8,128)S(1)}, f32[8,128]{1,0:T(8,128)S(1)}, u32[]{:S(2)}, u32[]{:S(2)}) collective-permute-start(f32[8,128]{1,0:T(8,128)S(1)} %match.1), channel_id=1, source_target_pairs={{0,32},{32,0},{64,96},{96,64},{128,160},{160,128},{192,224},{224,1... | collective-permute-start | bytes 12296 | tf_op jit(solution)/shard_map/ppermute | solution.py:377
  23.3 0.0 collective-permute-done.3
  23.3 1.1 %collective-permute-done.4 = f32[8,128]{1,0:T(8,128)S(1)} collective-permute-done((f32[8,128]{1,0:T(8,128)S(1)}, f32[8,128]{1,0:T(8,128)S(1)}, u32[]{:S(2)}, u32[]{:S(2)}) %collective-permute-start.4) | collective-permute-done | bytes 4128 | tf_op jit(solution)/shard_map/ppermute | solution.py:377
  24.5 12.2 %all_to_all.10 = f32[32,8,128]{2,1,0:T(8,128)S(1)} all-to-all(f32[32,8,128]{2,1,0:T(8,128)S(1)} %broadcast_in_dim.7), channel_id=1, replica_groups={{22,1,2,3,4,5,6,7,8,9,10,11,12,13,14,15,16,17,18,19,20,21,0,23,24,25,26..., dimensions={0} | all-to-all | bytes 262144 | tf_op jit(solution)/shard_map/all_to_all | solution.py:382
  36.6 1.3 %relax.1 = (f32[16,1,128]{2,1,0:T(1,128)S(1)}, f32[16,128]{1,0:T(8,128)S(1)}) custom-call(f32[256,128]{1,0:T(8,128)S(1)} %bitcast.2), custom_call_target="tpu_custom_call" | custom-call | tf_op jit(solution)/shard_map/relax/pallas_call | solution.py:390
  38.0 18.1 %all_to_all.11.sums = f32[16,1,128]{2,1,0:T(1,128)S(1)} all-to-all(f32[16,1,128]{2,1,0:T(1,128)S(1)} %get-tuple-element.18), channel_id=1, replica_groups={{256,288,320,352,384,416,448,480,0,32,64,96,128,160,192,224},{257,289,3..., dimensions={0} | all-to-all | bytes 16384 | tf_op jit(solution)/shard_map/all_to_all | solution.py:406
  56.0 0.7 %finish.1 = (f32[2,2,1,32]{3,2,1,0:T(1,128)}, f32[2,1,32]{2,1,0:T(1,128)}) custom-call(f32[16,1,128]{2,1,0:T(1,128)S(1)} %all_to_all.11.sums, f32[16,128]{1,0:T(8,128)S(1)} %get-tuple-element.19.fields), custom_call_target="tpu_custom_call" | custom-call | tf_op jit(solution)/shard_map/finish/pallas_call | solution.py:407
  (7 shorter events, 0.1 us)
Async XLA Ops:
  0.6 15.7 %collective-permute-start.2 = (bf16[32,4096]{1,0:T(8,128)(2,1)}, bf16[32,4096]{1,0:T(8,128)(2,1)S(1)}, u32[]{:S(2)}, u32[]{:S(2)}) collective-permute-start(bf16[32,4096]{1,0:T(8,128)(2,1)} %bitcast.3), channel_id=1, source_target_pairs={{0,8},{4,12},{8,16},{12,20},{16,24},{20,28},{24,32},{28,36},{32,40... | collective-permute-start | bytes 786440 | tf_op jit(solution)/shard_map/ppermute | solution.py:344
  5.8 9.2 %collective-permute-start = (bf16[32,3072]{1,0:T(8,128)(2,1)S(1)}, bf16[32,3072]{1,0:T(8,128)(2,1)S(1)}, u32[]{:S(2)}, u32[]{:S(2)}) collective-permute-start(bf16[32,3072]{1,0:T(8,128)(2,1)S(1)} %get-tuple-element.11), channel_id=1, source_target_pairs={{0,4},{4,0},{1,5},{5,1},{2,6},{6,2},{3,7},{7,3},{8,12},{12,8},{9,1... | collective-permute-start | bytes 589832 | tf_op jit(solution)/shard_map/ppermute | solution.py:359
  11.8 3.2 %collective-permute-start.1 = (bf16[32,1280]{1,0:T(8,128)(2,1)S(1)}, bf16[32,1280]{1,0:T(8,128)(2,1)S(1)}, u32[]{:S(2)}, u32[]{:S(2)}) collective-permute-start(bf16[32,1280]{1,0:T(8,128)(2,1)S(1)} %get-tuple-element.12), channel_id=1, source_target_pairs={{0,4},{4,0},{1,5},{5,1},{2,6},{6,2},{3,7},{7,3},{8,12},{12,8},{9,1... | collective-permute-start | bytes 245768 | tf_op jit(solution)/shard_map/ppermute | solution.py:359
  15.2 1.1 %copy-start = (f32[3,32,4096]{2,1,0:T(8,128)}, f32[3,32,4096]{2,1,0:T(8,128)S(1)}, u32[]{:S(2)}) copy-start(f32[3,32,4096]{2,1,0:T(8,128)S(1)} %get-tuple-element.14.faces) | copy-start | bytes 4718596
  16.3 1.4 %copy-start.1 = (f32[3,32,4096]{2,1,0:T(8,128)S(1)}, f32[3,32,4096]{2,1,0:T(8,128)}, u32[]{:S(2)}) copy-start(f32[3,32,4096]{2,1,0:T(8,128)} %copy-done) | copy-start | bytes 4718596
  19.4 3.9 %collective-permute-start.3 = (f32[8,128]{1,0:T(8,128)S(1)}, f32[8,128]{1,0:T(8,128)S(1)}, u32[]{:S(2)}, u32[]{:S(2)}) collective-permute-start(f32[8,128]{1,0:T(8,128)S(1)} %match.1), channel_id=1, source_target_pairs={{32,64},{64,32},{96,128},{128,96},{160,192},{192,160},{224,256},{2... | collective-permute-start | bytes 12296 | tf_op jit(solution)/shard_map/ppermute | solution.py:376
  20.0 4.4 %collective-permute-start.4 = (f32[8,128]{1,0:T(8,128)S(1)}, f32[8,128]{1,0:T(8,128)S(1)}, u32[]{:S(2)}, u32[]{:S(2)}) collective-permute-start(f32[8,128]{1,0:T(8,128)S(1)} %match.1), channel_id=1, source_target_pairs={{0,32},{32,0},{64,96},{96,64},{128,160},{160,128},{192,224},{224,1... | collective-permute-start | bytes 12296 | tf_op jit(solution)/shard_map/ppermute | solution.py:377
